TPU v7x, 512 devices: a whole 4x4x16 slice. The times are simulated.
512 devices in a mesh: row: 16 (over x, z_lo), col: 32 (over z_hi, y, core).
Axes of the slice: x: 4, y: 4, z: 16 (z_hi: 4, z_lo: 4; z = z_hi * 4 + z_lo), core: 2. Of those that a mesh axis runs over, the one named last changes fastest.
Arguments:
- covariance: float32 [16384, 16384], P('row', 'col')
- angles: float32 [3, 8192], replicated, may hold values from 0.3 to 1.3
- delays: int32 [3], replicated, may hold values from 128 to 8192, as said below
- panel: int32 [1], replicated, may hold values from 0 to 8064
Outputs:
- conditioned: float32 [16384, 16384], P('row', 'col')
Inputs may be any that keep to these rules, and one draw needn't show every extreme that they name: `delays`: each delay is 128 times a power of two; one of the three is 128, one is 8192.
All inputs are finite; a program needn't handle non-finite values.
Results may differ from a plain program's by a relative error of at most 0.000094.
Values sent between devices are 32-bit elements; how exact they have to be, the bound alone decides.
No kernel may reach another device: no remote copies, remote signals or barrier semaphores. Data moves between devices by JAX's collectives and lax.ppermute only.
A program may use at most 64 MiB of HBM per device.

v0:
```python
import functools

import jax
import jax.numpy as jnp
from jax import lax
from jax.experimental import pallas as pl
from jax.experimental.pallas import tpu as pltpu
from jax.sharding import PartitionSpec as P

PANEL = 128
QUANTUM = 128
HIGHEST = lax.Precision.HIGHEST
VMEM = pl.BlockSpec(memory_space=pltpu.VMEM)
SMEM = pl.BlockSpec(memory_space=pltpu.SMEM)


def swap(value, axis, mask):
    pairs = [(source, source ^ mask) for source in range(lax.axis_size(axis))]
    return lax.ppermute(value, axis, pairs)


class Plan:
    def __init__(self, level, top, row_blocks, col_blocks):
        self.gens = sorted({1, 1 << level, top})
        self.third = 1 << level
        self.top = top
        self.count = 1 << len(self.gens)
        self.top_bit = 1 << self.gens.index(top)
        self.third_bit = 1 << self.gens.index(self.third)
        self.values = [
            sum(g for k, g in enumerate(self.gens) if m >> k & 1) for m in range(self.count)
        ]
        self.row_blocks = row_blocks
        self.col_blocks = col_blocks
        inner = self.third not in (1, top)
        self.row_far = inner and self.third >= row_blocks
        self.col_far = inner and self.third >= col_blocks


def coefficients_kernel(plan, info, angles, out):
    count, top = plan.count, plan.top
    rows = 16 * count
    rid = lax.broadcasted_iota(jnp.int32, (rows, top), 0)
    lane = lax.broadcasted_iota(jnp.int32, (rows, top), 1)
    slot = rid & 15
    base = jnp.where(slot < 8, info[3] + slot, info[4] + (slot & (plan.col_blocks - 1)))
    mask = jnp.zeros_like(rid)
    for k, g in enumerate(plan.gens):
        mask = mask | (((rid >> (4 + k)) & 1) * g)
    block = base ^ mask
    own, other, delays = [], [], []
    for section in range(3):
        d = info[section]
        source = (block & ~d) & (top - 1)
        pick = (source == lane).astype(jnp.float32)
        theta = angles[section * top : (section + 1) * top, :]
        low = (block[:, :1] & d) == 0
        cos = jnp.dot(pick, jnp.cos(theta), precision=HIGHEST, preferred_element_type=jnp.float32)
        sin = jnp.dot(pick, jnp.sin(theta), precision=HIGHEST, preferred_element_type=jnp.float32)
        sin = jnp.where(low, -sin, sin)
        own.append([cos[16 * m : 16 * m + 16] for m in range(count)])
        other.append([sin[16 * m : 16 * m + 16] for m in range(count)])
        delays.append(d)

    def partner(values, d, m):
        result = values[m ^ 1]
        for k, g in enumerate(plan.gens[1:], 1):
            result = jnp.where(d == g, values[m ^ (1 << k)], result)
        return result

    one = jnp.ones((16, 128), jnp.float32)
    zero = jnp.zeros((16, 128), jnp.float32)

    def row_of(start):
        values = [one if m == start else zero for m in range(count)]
        for section in (2, 1, 0):
            a, b, d = own[section], other[section], delays[section]
            scaled = [values[m] * b[m] for m in range(count)]
            values = [values[m] * a[m] + partner(scaled, d, m) for m in range(count)]
        return values

    def col_of():
        values = [one if m == 0 else zero for m in range(count)]
        for section in (0, 1, 2):
            a, b, d = own[section], other[section], delays[section]
            values = [values[m] * a[m] + b[m] * partner(values, d, m) for m in range(count)]
        return values

    for n, values in enumerate(
        (row_of(0), row_of(plan.top_bit), col_of(), row_of(plan.third_bit))
    ):
        for m in range(count):
            out[n, m] = values[m]


def coefficients(plan, info, angles):
    return pl.pallas_call(
        functools.partial(coefficients_kernel, plan),
        out_shape=jax.ShapeDtypeStruct((4, plan.count, 16, 128), jnp.float32),
        in_specs=[SMEM, VMEM],
        out_specs=VMEM,
        compiler_params=pltpu.CompilerParams(vmem_limit_bytes=32 * 2**20),
    )(info, angles)


def row_kernel(plan, height, near_ref, top_ref, coef_ref, *outs):
    tables = [coef_ref[0], coef_ref[3]] if plan.row_far else [coef_ref[0]]
    blocks = height // 128
    far = plan.third_bit if plan.row_far else 0
    for which, out in enumerate(outs):
        table = tables[which]
        columns = [jnp.transpose(table[m, :8, :]) for m in range(plan.count)]
        for j in range(blocks):
            total = None
            for m in range(plan.count):
                if m & far:
                    continue
                ref = top_ref if m & plan.top_bit else near_ref
                value = plan.values[m] & ~plan.top
                i = j ^ value
                term = ref[128 * i : 128 * i + 128, :] * columns[m][:, j : j + 1]
                total = term if total is None else total + term
            out[128 * j : 128 * j + 128, :] = total


def mix_rows(plan, near, top, coef, width=128):
    height, all_width = near.shape
    n_out = 2 if plan.row_far else 1
    block = pl.BlockSpec((height, width), lambda i: (0, i))
    shape = jax.ShapeDtypeStruct(near.shape, jnp.float32)
    return pl.pallas_call(
        functools.partial(row_kernel, plan, height),
        grid=(all_width // width,),
        out_shape=[shape] * n_out,
        in_specs=[block, block, VMEM],
        out_specs=[block] * n_out,
        compiler_params=pltpu.CompilerParams(vmem_limit_bytes=48 * 2**20),
    )(near, top, coef)


def col_kernel(plan, *refs):
    if plan.col_far:
        near_ref, far_ref, coef_ref, mine, theirs = refs
    else:
        near_ref, coef_ref, mine, theirs = refs
        far_ref = None
    far = plan.third_bit if plan.col_far else 0
    for which, out in enumerate((mine, theirs)):
        for j in range(plan.col_blocks):
            total = None
            for m in range(plan.count):
                if m & plan.top_bit:
                    continue
                ref = far_ref if m & far else near_ref
                value = plan.values[m] & ~(plan.third if m & far else 0)
                i = j ^ value
                term = ref[:, 128 * i : 128 * i + 128] * coef_ref[which, m, 8 + j : 9 + j, :]
                total = term if total is None else total + term
            out[:, 128 * j : 128 * j + 128] = total


def mix_cols(plan, parts, coef, strip=128):
    height, width = parts[0].shape
    block = pl.BlockSpec((strip, width), lambda i: (i, 0))
    shape = jax.ShapeDtypeStruct((height, width), jnp.float32)
    return pl.pallas_call(
        functools.partial(col_kernel, plan),
        grid=(height // strip,),
        out_shape=[shape] * 2,
        in_specs=[block] * len(parts) + [VMEM],
        out_specs=[block] * 2,
        compiler_params=pltpu.CompilerParams(vmem_limit_bytes=48 * 2**20),
    )(*parts, coef)


def selection(plan, coef, base, n_blocks, first, panel, modes):
    n = n_blocks * QUANTUM
    ids = base * QUANTUM + jnp.arange(n, dtype=jnp.int32)
    slots = jnp.arange(2 * PANEL, dtype=jnp.int32)
    chosen = jnp.where(slots < PANEL, panel + slots, modes + panel + slots - PANEL)
    result = jnp.zeros((2 * PANEL, n), jnp.float32)
    for m in range(plan.count):
        at = ids ^ (plan.values[m] * QUANTUM)
        weight = coef[2, m, first : first + n_blocks].reshape(n)
        result = result + jnp.where(at[None, :] == chosen[:, None], weight[None, :], 0.0)
    return result


def gather_four(value, axis, unit):
    place = lax.axis_index(axis) // unit % 4
    result = jnp.zeros((4,) + value.shape, value.dtype)
    moved = [value] + [swap(value, axis, unit * k) for k in (1, 2, 3)]
    for k, piece in enumerate(moved):
        result = lax.dynamic_update_slice(result, piece[None], (place ^ k,) + (0,) * value.ndim)
    return result


def transposed(value):
    n_row, n_col = lax.axis_size("row"), lax.axis_size("col")
    pairs = []
    for r in range(n_row):
        for c in range(n_col):
            pairs.append((r * n_col + c, (c // 2) * n_col + r * 2 + c % 2))
    return lax.ppermute(value, ("row", "col"), pairs)


def panel_rows(plan, covariance, coef, rb, cb, panel, modes):
    rows_dev, cols_dev = covariance.shape
    n_row = lax.axis_size("row")
    sel_r = selection(plan, coef, rb, plan.row_blocks, 0, panel, modes)
    sel_c = selection(plan, coef, cb, plan.col_blocks, 8, panel, modes)
    part = jnp.dot(sel_r, covariance, precision=HIGHEST)
    each = 2 * PANEL // n_row
    spread = lax.all_to_all(part.reshape(n_row, each, cols_dev), "row", 0, 0)
    piece = jnp.sum(spread, axis=0)
    block = jnp.dot(piece, sel_c.T, precision=HIGHEST)
    block = block + swap(block, "col", 1)
    block = sum([swap(block, "col", 2 * k) for k in (1, 2, 3)], block)
    block = sum([swap(block, "col", 8 * k) for k in (1, 2, 3)], block)
    moved = {0: piece, plan.top_bit: swap(piece, "col", plan.top // plan.col_blocks)}
    if plan.col_far:
        mask = plan.third // plan.col_blocks
        moved[plan.third_bit] = swap(piece, "col", mask)
        both = mask ^ (plan.top // plan.col_blocks)
        moved[plan.third_bit | plan.top_bit] = swap(piece, "col", both)
    far = plan.top_bit | (plan.third_bit if plan.col_far else 0)
    far_value = plan.top | (plan.third if plan.col_far else 0)
    mixed = []
    for j in range(plan.col_blocks):
        total = 0.0
        for m in range(plan.count):
            i = j ^ (plan.values[m] & ~far_value)
            source = moved[m & far][:, 128 * i : 128 * i + 128]
            total = total + source * coef[0, m, 8 + j][None, :]
        mixed.append(total)
    mixed = jnp.concatenate(mixed, axis=1)
    return block, mixed


def branch(level, covariance, angles, delays, panel):
    rows_dev, cols_dev = covariance.shape
    n_row, n_col = lax.axis_size("row"), lax.axis_size("col")
    modes = rows_dev * n_row // 2
    top = modes // QUANTUM
    plan = Plan(level, top, rows_dev // QUANTUM, cols_dev // QUANTUM)
    row_top = top // plan.row_blocks
    rb = lax.axis_index("row").astype(jnp.int32) * plan.row_blocks
    cb = lax.axis_index("col").astype(jnp.int32) * plan.col_blocks
    info = jnp.concatenate([delays // QUANTUM, rb[None], cb[None]]).astype(jnp.int32)
    coef = coefficients(plan, info, angles.reshape(3 * top, QUANTUM))
    over = swap(covariance, "row", row_top)

    block, mixed = panel_rows(plan, covariance, coef, rb, cb, panel, modes)

    if plan.row_far:
        mine, theirs = mix_rows(plan, covariance, over, coef)
        field = mine + swap(theirs, "row", plan.third // plan.row_blocks)
    else:
        (field,) = mix_rows(plan, covariance, over, coef)
    parts = [field]
    if plan.col_far:
        parts.append(swap(field, "col", plan.third // plan.col_blocks))
    mine, theirs = mix_cols(plan, parts, coef)
    arrived = swap(theirs, "col", top // plan.col_blocks)

    each = mixed.shape[0]
    both = jnp.concatenate([mixed, block], axis=1)
    both = lax.all_to_all(jnp.broadcast_to(both[None], (n_row,) + both.shape), "row", 0, 0)
    both = both.reshape(2 * PANEL, -1)
    rows_part, square = both[:, :cols_dev], both[:, cols_dev:]
    flipped = transposed(mixed)
    flipped = gather_four(flipped, "col", 8)
    flipped = gather_four(flipped, "col", 2)
    core = lax.axis_index("col") % 2
    twin = swap(flipped, "col", 1)
    pair = jnp.zeros(flipped.shape[:3] + (2, cols_dev), jnp.float32)
    pair = lax.dynamic_update_slice(pair, flipped[:, :, :, None], (0, 0, 0, core, 0))
    pair = lax.dynamic_update_slice(pair, twin[:, :, :, None], (0, 0, 0, 1 - core, 0))
    columns = pair.transpose(1, 0, 2, 3, 4).reshape(2 * PANEL, rows_dev)

    factor = jnp.linalg.cholesky(square)
    half = lax.linalg.triangular_solve(factor, rows_part, left_side=True, lower=True)
    weights = lax.linalg.triangular_solve(
        factor, half, left_side=True, lower=True, transpose_a=True
    )
    update = lax.dot_general(columns, weights, (((0,), (0,)), ((), ())), precision=HIGHEST)
    return mine + arrived - update


def shards(covariance, angles, delays, panel):
    rows_dev = covariance.shape[0]
    modes = rows_dev * lax.axis_size("row") // 2
    levels = (modes // QUANTUM).bit_length()
    third = jnp.sum(delays) - modes - QUANTUM
    level = jnp.int32(0)
    for n in range(1, levels):
        level = level + (third >= QUANTUM * (1 << n)).astype(jnp.int32)
    branches = [functools.partial(branch, n) for n in range(levels)]
    return lax.switch(level, branches, covariance, angles, delays, panel[0])


def solution(mesh):
    in_specs = (P("row", "col"), P(), P(), P())
    out_specs = P("row", "col")
    return jax.shard_map(shards, mesh=mesh, in_specs=in_specs, out_specs=out_specs, check_vma=False)
```

profile of v0, /device:TPU:23, one launch (start us, length us, event | category | flops | bytes accessed | tf_op | source)
XLA Modules:
  0.0 497.9 jit_solution(3394713667644546183)
XLA Ops:
  2.0 494.1 %conditional.1 = (f32[1024,512]{1,0:T(8,128)S(1)}) conditional(s32[]{:T(128)} %clamp.3, (f32[1024,512]{1,0:T(8,128)}, s32[3]{0:T(128)}, f32[3,8192]{1,0:T(4,128)}, s32[1]{0:T(128)}) %tuple.29, (f32[1024,512]{1,0:T(8,128)}, s32[3]{0:T(128)}, f32[3,8192]{1,0:T(4,128)}, s32[1]{0:T(128)}) %tuple.29, ...), branch_computations={%region_1.10_spmd, %region_7.12_spmd, %region_9.14_spmd, %region_1... | conditional | flops 3912439808 | bytes 98885024 | solution.py:299
  13.6 5.3 %fusion.300 = f32[256,512]{1,0:T(8,128)} fusion(f32[1024,512]{1,0:T(8,128)} %get-tuple-element.145.near_ref, f32[1024]{0:T(1024)S(1)} %get-tuple-element.617, s32[1024]{0:T(1024)S(1)} %get-tuple-element.631, f32[1024]{0:T(1024)S(1)} %get-tuple-element.618, s32[1024]{0:T(1024)S(1)} %get-tuple-element.632, f32[1024]{0:T(1024)S(1)} %get-tuple-element.619, ...), kind=kOutput, calls=%fused_computation.570 | convolution fusion | flops 1616642048 | bytes 2688000 | tf_op jit(solution)/shard_map/cond/branch_3_fun/dot_general | solution.py:212
  18.9 8.3 %all-to-all-start.6 = ((f32[16,16,512]{2,1,0:T(8,128)}), f32[16,16,512]{2,1,0:T(8,128)S(1)}, u32[]{:S(2)}, u32[]{:S(2)}) async-start(f32[16,16,512]{2,1,0:T(8,128)} %bitcast.1178), calls=%async_computation.6 | async-start | bytes 1048576 | tf_op jit(solution)/shard_map/cond/branch_3_fun/all_to_all | solution.py:214
  27.2 3.1 collective-permute-start.62
  30.4 10.9 %all-to-all-done.6 = f32[16,16,512]{2,1,0:T(8,128)S(1)} async-done(((f32[16,16,512]{2,1,0:T(8,128)}), f32[16,16,512]{2,1,0:T(8,128)S(1)}, u32[]{:S(2)}, u32[]{:S(2)}) %all-to-all-start.6) | async-done | bytes 524320 | tf_op jit(solution)/shard_map/cond/branch_3_fun/all_to_all | solution.py:214
  42.3 3.4 collective-permute-start.77
  48.5 4.5 collective-permute-start.79
  55.4 13.5 %collective-permute-start.68 = (f32[16,512]{1,0:T(8,128)S(1)}, f32[16,512]{1,0:T(8,128)S(1)}, u32[]{:S(2)}, u32[]{:S(2)}) collective-permute-start(f32[16,512]{1,0:T(8,128)S(1)} %reduce_sum.67), channel_id=1, source_target_pairs={{0,18},{1,19},{2,16},{3,17},{4,22},{5,23},{6,20},{7,21},{8,26},{9,... | collective-permute-start | bytes 98312 | tf_op jit(solution)/shard_map/cond/branch_3_fun/ppermute | solution.py:19
  73.3 9.1 %collective-permute-start.83 = (f32[16,256]{1,0:T(8,128)S(1)}, f32[16,256]{1,0:T(8,128)S(1)}, u32[]{:S(2)}, u32[]{:S(2)}) collective-permute-start(f32[16,256]{1,0:T(8,128)S(1)} %add_add_fusion.3), channel_id=1, source_target_pairs={{0,24},{1,25},{2,26},{3,27},{4,28},{5,29},{6,30},{7,31},{8,16},{9,... | collective-permute-start | bytes 49160 | tf_op jit(solution)/shard_map/cond/branch_3_fun/ppermute | solution.py:19
  82.4 6.1 %collective-permute-start.82 = (f32[16,256]{1,0:T(8,128)S(1)}, f32[16,256]{1,0:T(8,128)S(1)}, u32[]{:S(2)}, u32[]{:S(2)}) collective-permute-start(f32[16,256]{1,0:T(8,128)S(1)} %add_add_fusion.3), channel_id=1, source_target_pairs={{0,16},{1,17},{2,18},{3,19},{4,20},{5,21},{6,22},{7,23},{8,24},{9,... | collective-permute-start | bytes 49160 | tf_op jit(solution)/shard_map/cond/branch_3_fun/ppermute | solution.py:19
  91.4 4.1 collective-permute-done.82
  98.3 5.7 %all-to-all-start.7 = ((f32[16,16,768]{2,1,0:T(8,128)}), f32[16,16,768]{2,1,0:T(8,128)S(1)}, u32[]{:S(2)}, u32[]{:S(2)}) async-start(f32[16,16,768]{2,1,0:T(8,128)} %broadcast_in_dim.1165), calls=%async_computation.7 | async-start | bytes 1572864 | tf_op jit(solution)/shard_map/cond/branch_3_fun/all_to_all | solution.py:268
  104.0 7.7 %branch_3_fun.4 = (f32[1024,512]{1,0:T(8,128)S(1)}, f32[1024,512]{1,0:T(8,128)}) custom-call(f32[1024,512]{1,0:T(8,128)} %get-tuple-element.145.near_ref, f32[1024,512]{1,0:T(8,128)} %collective-permute-done.62.top_ref, f32[4,8,16,128]{3,2,1,0:T(8,128)S(1)} %branch_3_fun.3.coef_ref.refs_2_), custom_call_target="tpu_custom_call" | custom-call | tf_op jit(solution)/shard_map/cond/branch_3_fun/pallas_call | solution.py:131
  111.7 3.1 collective-permute-start.63
  114.8 5.6 %collective-permute-start.69 = (f32[16,512]{1,0:T(8,128)S(1)}, f32[16,512]{1,0:T(8,128)S(1)}, u32[]{:S(2)}, u32[]{:S(2)}) collective-permute-start(f32[16,512]{1,0:T(8,128)S(1)} %pad_maximum_fusion.3), channel_id=1, source_target_pairs={{0,0},{1,1},{2,32},{3,33},{4,64},{5,65},{6,96},{7,97},{8,128},{9,1... | collective-permute-start | bytes 98312 | tf_op jit(solution)/shard_map/cond/branch_3_fun/ppermute | solution.py:204
  120.5 47.2 %collective-permute-done.69 = f32[16,512]{1,0:T(8,128)S(1)} collective-permute-done((f32[16,512]{1,0:T(8,128)S(1)}, f32[16,512]{1,0:T(8,128)S(1)}, u32[]{:S(2)}, u32[]{:S(2)}) %collective-permute-start.69) | collective-permute-done | bytes 32800 | tf_op jit(solution)/shard_map/cond/branch_3_fun/ppermute | solution.py:204
  169.6 12.0 %collective-permute-start.71 = (f32[16,512]{1,0:T(8,128)S(1)}, f32[16,512]{1,0:T(8,128)S(1)}, u32[]{:S(2)}, u32[]{:S(2)}) collective-permute-start(f32[16,512]{1,0:T(8,128)S(1)} %collective-permute-done.69), channel_id=1, source_target_pairs={{0,16},{1,17},{2,18},{3,19},{4,20},{5,21},{6,22},{7,23},{8,24},{9,... | collective-permute-start | bytes 98312 | tf_op jit(solution)/shard_map/cond/branch_3_fun/ppermute | solution.py:19
  183.9 6.3 %collective-permute-done.70 = f32[16,512]{1,0:T(8,128)S(1)} collective-permute-done((f32[16,512]{1,0:T(8,128)S(1)}, f32[16,512]{1,0:T(8,128)S(1)}, u32[]{:S(2)}, u32[]{:S(2)}) %collective-permute-start.70) | collective-permute-done | bytes 32800 | tf_op jit(solution)/shard_map/cond/branch_3_fun/ppermute | solution.py:19
  194.2 5.1 %collective-permute-start.73 = (f32[4,16,512]{2,1,0:T(8,128)S(1)}, f32[4,16,512]{2,1,0:T(8,128)S(1)}, u32[]{:S(2)}, u32[]{:S(2)}) collective-permute-start(f32[4,16,512]{2,1,0:T(8,128)S(1)} %bitcast_dynamic-update-slice_fusion.32), channel_id=1, source_target_pairs={{0,2},{1,3},{2,0},{3,1},{4,6},{5,7},{6,4},{7,5},{8,10},{9,11},{10,... | collective-permute-start | bytes 393224 | tf_op jit(solution)/shard_map/cond/branch_3_fun/ppermute | solution.py:19
  203.3 3.4 add.1599.refs_0_
  206.7 3.8 collective-permute-start.64
  211.1 8.8 %collective-permute-start.76 = (f32[4,4,16,512]{3,2,0,1:T(8,128)}, f32[4,4,16,512]{3,2,0,1:T(8,128)S(1)}, u32[]{:S(2)}, u32[]{:S(2)}) collective-permute-start(f32[4,4,16,512]{3,2,0,1:T(8,128)} %bitcast_dynamic-update-slice_fusion.31), channel_id=1, source_target_pairs={{0,1},{1,0},{2,3},{3,2},{4,5},{5,4},{6,7},{7,6},{8,9},{9,8},{10,11... | collective-permute-start | bytes 1572872 | tf_op jit(solution)/shard_map/cond/branch_3_fun/ppermute | solution.py:19
  222.0 4.6 dynamic_update_slice.178
  227.1 4.5 dynamic_update_slice.179
  233.0 11.7 %cholesky.442 = f32[128,128]{1,0:T(8,128)S(1)} custom-call(f32[128,128]{1,0:T(8,128)S(1)} %cholesky.583), custom_call_target="Cholesky" | custom-call | tf_op jit(solution)/shard_map/cond/branch_3_fun/jit(cholesky)/cholesky | solution.py:281
  244.8 9.8 %custom-call.41 = f32[1,128,128]{1,2,0:T(8,128)S(1)} custom-call(f32[1,128,128]{2,1,0:T(8,128)S(1)} %get-tuple-element.627), custom_call_target="InvertDiagBlocksLowerTriangular" | custom-call | tf_op jit(solution)/shard_map/cond/branch_3_fun/jit(cholesky)/cholesky | solution.py:281
  255.1 11.7 %cholesky.459 = f32[128,128]{1,0:T(8,128)S(1)} custom-call(f32[128,128]{1,0:T(8,128)S(1)} %convolution_subtract_fusion.11), custom_call_target="Cholesky" | custom-call | tf_op jit(solution)/shard_map/cond/branch_3_fun/jit(cholesky)/cholesky | solution.py:281
  269.5 6.2 %branch_3_fun.5 = (f32[1024,512]{1,0:T(8,128)S(1)}, f32[1024,512]{1,0:T(8,128)}) custom-call(f32[1024,512]{1,0:T(8,128)} %add.1599.refs_0_, f32[1024,512]{1,0:T(8,128)} %collective-permute-done.64.refs_1_, f32[4,8,16,128]{3,2,1,0:T(8,128)S(1)} %branch_3_fun.3.coef_ref.refs_2_), custom_call_target="tpu_custom_call" | custom-call | tf_op jit(solution)/shard_map/cond/branch_3_fun/pallas_call | solution.py:166
  275.7 4.2 collective-permute-start.65
  280.0 4.2 while.31
  284.1 19.7 %custom-call.43 = f32[2,128,128]{1,2,0:T(8,128)S(1)} custom-call(f32[2,128,128]{2,1,0:T(8,128)S(1)} %get-tuple-element.265), custom_call_target="InvertDiagBlocksLowerTriangular" | custom-call | tf_op jit(solution)/shard_map/cond/branch_3_fun/triangular_solve/custom-call.4 | solution.py:283
  308.1 160.9 %collective-permute-done.65 = f32[1024,512]{1,0:T(8,128)} collective-permute-done((f32[1024,512]{1,0:T(8,128)}, f32[1024,512]{1,0:T(8,128)}, u32[]{:S(2)}, u32[]{:S(2)}) %collective-permute-start.65) | collective-permute-done | bytes 2097184 | tf_op jit(solution)/shard_map/cond/branch_3_fun/ppermute | solution.py:19
  (106 shorter events, 51.6 us)
Async XLA Ops:
  13.6 13.6 %copy-start.6 = (f32[1024,512]{1,0:T(8,128)S(1)}, f32[1024,512]{1,0:T(8,128)}, u32[]{:S(2)}) copy-start(f32[1024,512]{1,0:T(8,128)} %get-tuple-element.145.near_ref) | copy-start | bytes 6291460 | tf_op jit(solution)/shard_map/cond
  18.9 22.4 %all-to-all-start.6 = ((f32[16,16,512]{2,1,0:T(8,128)}), f32[16,16,512]{2,1,0:T(8,128)S(1)}, u32[]{:S(2)}, u32[]{:S(2)}) async-start(f32[16,16,512]{2,1,0:T(8,128)} %bitcast.1178), calls=%async_computation.6 | async-start | bytes 1048576 | tf_op jit(solution)/shard_map/cond/branch_3_fun/all_to_all | solution.py:214
  27.2 76.8 %collective-permute-start.62 = (f32[1024,512]{1,0:T(8,128)S(1)}, f32[1024,512]{1,0:T(8,128)}, u32[]{:S(2)}, u32[]{:S(2)}) collective-permute-start(f32[1024,512]{1,0:T(8,128)S(1)} %copy-done.6), channel_id=1, source_target_pairs={{0,256},{32,288},{64,320},{96,352},{128,384},{160,416},{192,448},{... | collective-permute-start | bytes 6291464 | tf_op jit(solution)/shard_map/cond/branch_3_fun/ppermute | solution.py:19
  42.3 4.2 collective-permute-start.77
  46.4 22.5 %collective-permute-start.80 = (f32[16,256]{1,0:T(8,128)S(1)}, f32[16,256]{1,0:T(8,128)S(1)}, u32[]{:S(2)}, u32[]{:S(2)}) collective-permute-start(f32[16,256]{1,0:T(8,128)S(1)} %add.1665), channel_id=1, source_target_pairs={{0,6},{1,7},{2,4},{3,5},{4,2},{5,3},{6,0},{7,1},{8,14},{9,15},{10,... | collective-permute-start | bytes 49160 | tf_op jit(solution)/shard_map/cond/branch_3_fun/ppermute | solution.py:19
  48.5 22.4 %collective-permute-start.79 = (f32[16,256]{1,0:T(8,128)S(1)}, f32[16,256]{1,0:T(8,128)S(1)}, u32[]{:S(2)}, u32[]{:S(2)}) collective-permute-start(f32[16,256]{1,0:T(8,128)S(1)} %add.1665), channel_id=1, source_target_pairs={{0,4},{1,5},{2,6},{3,7},{4,0},{5,1},{6,2},{7,3},{8,12},{9,13},{10,... | collective-permute-start | bytes 49160 | tf_op jit(solution)/shard_map/cond/branch_3_fun/ppermute | solution.py:19
  53.1 20.2 %collective-permute-start.78 = (f32[16,256]{1,0:T(8,128)S(1)}, f32[16,256]{1,0:T(8,128)S(1)}, u32[]{:S(2)}, u32[]{:S(2)}) collective-permute-start(f32[16,256]{1,0:T(8,128)S(1)} %add.1665), channel_id=1, source_target_pairs={{0,2},{1,3},{2,0},{3,1},{4,6},{5,7},{6,4},{7,5},{8,10},{9,11},{10,... | collective-permute-start | bytes 49160 | tf_op jit(solution)/shard_map/cond/branch_3_fun/ppermute | solution.py:19
  55.4 26.9 %collective-permute-start.68 = (f32[16,512]{1,0:T(8,128)S(1)}, f32[16,512]{1,0:T(8,128)S(1)}, u32[]{:S(2)}, u32[]{:S(2)}) collective-permute-start(f32[16,512]{1,0:T(8,128)S(1)} %reduce_sum.67), channel_id=1, source_target_pairs={{0,18},{1,19},{2,16},{3,17},{4,22},{5,23},{6,20},{7,21},{8,26},{9,... | collective-permute-start | bytes 98312 | tf_op jit(solution)/shard_map/cond/branch_3_fun/ppermute | solution.py:19
  68.9 19.5 %collective-permute-start.67 = (f32[16,512]{1,0:T(8,128)S(1)}, f32[16,512]{1,0:T(8,128)S(1)}, u32[]{:S(2)}, u32[]{:S(2)}) collective-permute-start(f32[16,512]{1,0:T(8,128)S(1)} %reduce_sum.67), channel_id=1, source_target_pairs={{0,16},{1,17},{2,18},{3,19},{4,20},{5,21},{6,22},{7,23},{8,24},{9,... | collective-permute-start | bytes 98312 | tf_op jit(solution)/shard_map/cond/branch_3_fun/ppermute | solution.py:19
  70.9 20.4 %collective-permute-start.66 = (f32[16,512]{1,0:T(8,128)S(1)}, f32[16,512]{1,0:T(8,128)S(1)}, u32[]{:S(2)}, u32[]{:S(2)}) collective-permute-start(f32[16,512]{1,0:T(8,128)S(1)} %reduce_sum.67), channel_id=1, source_target_pairs={{0,2},{1,3},{2,0},{3,1},{4,6},{5,7},{6,4},{7,5},{8,10},{9,11},{10,... | collective-permute-start | bytes 98312 | tf_op jit(solution)/shard_map/cond/branch_3_fun/ppermute | solution.py:19
  73.3 18.1 %collective-permute-start.83 = (f32[16,256]{1,0:T(8,128)S(1)}, f32[16,256]{1,0:T(8,128)S(1)}, u32[]{:S(2)}, u32[]{:S(2)}) collective-permute-start(f32[16,256]{1,0:T(8,128)S(1)} %add_add_fusion.3), channel_id=1, source_target_pairs={{0,24},{1,25},{2,26},{3,27},{4,28},{5,29},{6,30},{7,31},{8,16},{9,... | collective-permute-start | bytes 49160 | tf_op jit(solution)/shard_map/cond/branch_3_fun/ppermute | solution.py:19
  82.4 13.2 %collective-permute-start.82 = (f32[16,256]{1,0:T(8,128)S(1)}, f32[16,256]{1,0:T(8,128)S(1)}, u32[]{:S(2)}, u32[]{:S(2)}) collective-permute-start(f32[16,256]{1,0:T(8,128)S(1)} %add_add_fusion.3), channel_id=1, source_target_pairs={{0,16},{1,17},{2,18},{3,19},{4,20},{5,21},{6,22},{7,23},{8,24},{9,... | collective-permute-start | bytes 49160 | tf_op jit(solution)/shard_map/cond/branch_3_fun/ppermute | solution.py:19
  88.5 8.8 %collective-permute-start.81 = (f32[16,256]{1,0:T(8,128)S(1)}, f32[16,256]{1,0:T(8,128)S(1)}, u32[]{:S(2)}, u32[]{:S(2)}) collective-permute-start(f32[16,256]{1,0:T(8,128)S(1)} %add_add_fusion.3), channel_id=1, source_target_pairs={{0,8},{1,9},{2,10},{3,11},{4,12},{5,13},{6,14},{7,15},{8,0},{9,1},... | collective-permute-start | bytes 49160 | tf_op jit(solution)/shard_map/cond/branch_3_fun/ppermute | solution.py:19
  98.3 134.5 %all-to-all-start.7 = ((f32[16,16,768]{2,1,0:T(8,128)}), f32[16,16,768]{2,1,0:T(8,128)S(1)}, u32[]{:S(2)}, u32[]{:S(2)}) async-start(f32[16,16,768]{2,1,0:T(8,128)} %broadcast_in_dim.1165), calls=%async_computation.7 | async-start | bytes 1572864 | tf_op jit(solution)/shard_map/cond/branch_3_fun/all_to_all | solution.py:268
  111.7 91.6 %collective-permute-start.63 = (f32[1024,512]{1,0:T(8,128)}, f32[1024,512]{1,0:T(8,128)}, u32[]{:S(2)}, u32[]{:S(2)}) collective-permute-start(f32[1024,512]{1,0:T(8,128)} %get-tuple-element.94), channel_id=1, source_target_pairs={{0,32},{32,0},{64,96},{96,64},{128,160},{160,128},{192,224},{224,1... | collective-permute-start | bytes 6291464 | tf_op jit(solution)/shard_map/cond/branch_3_fun/ppermute | solution.py:19
  114.8 52.9 %collective-permute-start.69 = (f32[16,512]{1,0:T(8,128)S(1)}, f32[16,512]{1,0:T(8,128)S(1)}, u32[]{:S(2)}, u32[]{:S(2)}) collective-permute-start(f32[16,512]{1,0:T(8,128)S(1)} %pad_maximum_fusion.3), channel_id=1, source_target_pairs={{0,0},{1,1},{2,32},{3,33},{4,64},{5,65},{6,96},{7,97},{8,128},{9,1... | collective-permute-start | bytes 98312 | tf_op jit(solution)/shard_map/cond/branch_3_fun/ppermute | solution.py:204
  167.7 22.6 %collective-permute-start.72 = (f32[16,512]{1,0:T(8,128)S(1)}, f32[16,512]{1,0:T(8,128)S(1)}, u32[]{:S(2)}, u32[]{:S(2)}) collective-permute-start(f32[16,512]{1,0:T(8,128)S(1)} %collective-permute-done.69), channel_id=1, source_target_pairs={{0,24},{1,25},{2,26},{3,27},{4,28},{5,29},{6,30},{7,31},{8,16},{9,... | collective-permute-start | bytes 98312 | tf_op jit(solution)/shard_map/cond/branch_3_fun/ppermute | solution.py:19
  169.6 20.6 %collective-permute-start.71 = (f32[16,512]{1,0:T(8,128)S(1)}, f32[16,512]{1,0:T(8,128)S(1)}, u32[]{:S(2)}, u32[]{:S(2)}) collective-permute-start(f32[16,512]{1,0:T(8,128)S(1)} %collective-permute-done.69), channel_id=1, source_target_pairs={{0,16},{1,17},{2,18},{3,19},{4,20},{5,21},{6,22},{7,23},{8,24},{9,... | collective-permute-start | bytes 98312 | tf_op jit(solution)/shard_map/cond/branch_3_fun/ppermute | solution.py:19
  181.7 8.6 %collective-permute-start.70 = (f32[16,512]{1,0:T(8,128)S(1)}, f32[16,512]{1,0:T(8,128)S(1)}, u32[]{:S(2)}, u32[]{:S(2)}) collective-permute-start(f32[16,512]{1,0:T(8,128)S(1)} %collective-permute-done.69), channel_id=1, source_target_pairs={{0,8},{1,9},{2,10},{3,11},{4,12},{5,13},{6,14},{7,15},{8,0},{9,1},... | collective-permute-start | bytes 98312 | tf_op jit(solution)/shard_map/cond/branch_3_fun/ppermute | solution.py:19
  190.3 20.2 %collective-permute-start.75 = (f32[4,16,512]{2,1,0:T(8,128)S(1)}, f32[4,16,512]{2,1,0:T(8,128)S(1)}, u32[]{:S(2)}, u32[]{:S(2)}) collective-permute-start(f32[4,16,512]{2,1,0:T(8,128)S(1)} %bitcast_dynamic-update-slice_fusion.32), channel_id=1, source_target_pairs={{0,6},{1,7},{2,4},{3,5},{4,2},{5,3},{6,0},{7,1},{8,14},{9,15},{10,... | collective-permute-start | bytes 393224 | tf_op jit(solution)/shard_map/cond/branch_3_fun/ppermute | solution.py:19
  192.2 10.4 %collective-permute-start.74 = (f32[4,16,512]{2,1,0:T(8,128)S(1)}, f32[4,16,512]{2,1,0:T(8,128)S(1)}, u32[]{:S(2)}, u32[]{:S(2)}) collective-permute-start(f32[4,16,512]{2,1,0:T(8,128)S(1)} %bitcast_dynamic-update-slice_fusion.32), channel_id=1, source_target_pairs={{0,4},{1,5},{2,6},{3,7},{4,0},{5,1},{6,2},{7,3},{8,12},{9,13},{10,... | collective-permute-start | bytes 393224 | tf_op jit(solution)/shard_map/cond/branch_3_fun/ppermute | solution.py:19
  194.2 7.8 %collective-permute-start.73 = (f32[4,16,512]{2,1,0:T(8,128)S(1)}, f32[4,16,512]{2,1,0:T(8,128)S(1)}, u32[]{:S(2)}, u32[]{:S(2)}) collective-permute-start(f32[4,16,512]{2,1,0:T(8,128)S(1)} %bitcast_dynamic-update-slice_fusion.32), channel_id=1, source_target_pairs={{0,2},{1,3},{2,0},{3,1},{4,6},{5,7},{6,4},{7,5},{8,10},{9,11},{10,... | collective-permute-start | bytes 393224 | tf_op jit(solution)/shard_map/cond/branch_3_fun/ppermute | solution.py:19
  206.7 62.8 %collective-permute-start.64 = (f32[1024,512]{1,0:T(8,128)}, f32[1024,512]{1,0:T(8,128)}, u32[]{:S(2)}, u32[]{:S(2)}) collective-permute-start(f32[1024,512]{1,0:T(8,128)} %add.1599.refs_0_), channel_id=1, source_target_pairs={{0,2},{1,3},{2,0},{3,1},{4,6},{5,7},{6,4},{7,5},{8,10},{9,11},{10,... | collective-permute-start | bytes 6291464 | tf_op jit(solution)/shard_map/cond/branch_3_fun/ppermute | solution.py:19
  211.1 15.5 %collective-permute-start.76 = (f32[4,4,16,512]{3,2,0,1:T(8,128)}, f32[4,4,16,512]{3,2,0,1:T(8,128)S(1)}, u32[]{:S(2)}, u32[]{:S(2)}) collective-permute-start(f32[4,4,16,512]{3,2,0,1:T(8,128)} %bitcast_dynamic-update-slice_fusion.31), channel_id=1, source_target_pairs={{0,1},{1,0},{2,3},{3,2},{4,5},{5,4},{6,7},{7,6},{8,9},{9,8},{10,11... | collective-permute-start | bytes 1572872 | tf_op jit(solution)/shard_map/cond/branch_3_fun/ppermute | solution.py:19
  275.7 193.3 %collective-permute-start.65 = (f32[1024,512]{1,0:T(8,128)}, f32[1024,512]{1,0:T(8,128)}, u32[]{:S(2)}, u32[]{:S(2)}) collective-permute-start(f32[1024,512]{1,0:T(8,128)} %get-tuple-element.96), channel_id=1, source_target_pairs={{0,16},{1,17},{2,18},{3,19},{4,20},{5,21},{6,22},{7,23},{8,24},{9,... | collective-permute-start | bytes 6291464 | tf_op jit(solution)/shard_map/cond/branch_3_fun/ppermute | solution.py:19
  303.8 2.4 copy-start.10
  496.1 1.3 copy-start.16
where the time goes:
time: 505 us; the launch traced here: 498 us
  waiting for transfers between devices  233 us (46%)
  starting transfers between devices  116 us (23%)
  other arithmetic  63 us (12%)
  loops' own time  34.8 us (7%)
  local copies, waits for them, and re-layouts  23.8 us (5%)
  Pallas kernels  15.3 us (3%)
  matrix products  10.8 us (2%)
    ppermute x21, waiting for transfers between devices, swap(): return lax.ppermute(value, axis, pairs)  175 us
    ppermute x21, starting transfers between devices, swap(): return lax.ppermute(value, axis, pairs)  96.2 us
    ppermute x1, waiting for transfers between devices, transposed(): return lax.ppermute(value, ('row', 'col'), pairs)  47.2 us
    another operation x7, other arithmetic, branch(): factor = jnp.linalg.cholesky(square)  34.6 us
    another operation x1, loops' own time, shards(): return lax.switch(level, branches, covariance, angles, delays, panel[0])  34.5 us
    another operation x4, other arithmetic, branch(): lax.linalg.triangular_solve(factor, half, left_side=True, lower=True, tra...  19.7 us
    all_to_all x1, waiting for transfers between devices, panel_rows(): spread = lax.all_to_all(part.reshape(n_row, each, cols_dev), 'row', 0, 0)  10.9 us
  transfers between devices with their start and end apart: 24, of which 8 were waited for; matrix products, arithmetic and copies ran while one was open for 17% of the time, Pallas kernels for 2%

commit v1 on v0

v1 whole, which is shorter than its diff:
```python
import functools

import jax
import jax.numpy as jnp
from jax import lax
from jax.experimental import pallas as pl
from jax.experimental.pallas import tpu as pltpu
from jax.sharding import PartitionSpec as P

PANEL = 128
QUANTUM = 128
HIGHEST = lax.Precision.HIGHEST
VMEM = pl.BlockSpec(memory_space=pltpu.VMEM)
SMEM = pl.BlockSpec(memory_space=pltpu.SMEM)


def swap(value, axis, mask):
    pairs = [(source, source ^ mask) for source in range(lax.axis_size(axis))]
    return lax.ppermute(value, axis, pairs)


def swap_far(value, axis, third, thirds, per_device):
    if len(thirds) == 1:
        return swap(value, axis, thirds[0] // per_device)
    index = sum((third > t).astype(jnp.int32) for t in thirds[:-1])
    ways = [functools.partial(swap, axis=axis, mask=t // per_device) for t in thirds]
    return lax.switch(index, ways, value)


class Plan:
    count, third_bit, top_bit = 8, 2, 4

    def __init__(self, thirds, top, row_blocks, col_blocks):
        third = thirds[0]
        self.third, self.thirds, self.top = third, thirds, top
        self.values = [(m & 1) + (m >> 1 & 1) * third + (m >> 2) * top for m in range(self.count)]
        self.row_blocks = row_blocks
        self.col_blocks = col_blocks
        self.row_far = third >= row_blocks
        self.col_far = third >= col_blocks


def coefficients_kernel(count, top, col_blocks, info, angles, out):
    gens = (1, info[5], top)
    rows = 16 * count
    rid = lax.broadcasted_iota(jnp.int32, (rows, top), 0)
    lane = lax.broadcasted_iota(jnp.int32, (rows, top), 1)
    slot = rid & 15
    base = jnp.where(slot < 8, info[3] + slot, info[4] + (slot & (col_blocks - 1)))
    mask = jnp.zeros_like(rid)
    for k, g in enumerate(gens):
        mask = mask | (((rid >> (4 + k)) & 1) * g)
    block = base ^ mask
    own, other, delays = [], [], []
    for section in range(3):
        d = info[section]
        source = (block & ~d) & (top - 1)
        pick = (source == lane).astype(jnp.float32)
        theta = angles[section * top : (section + 1) * top, :]
        low = (block[:, :1] & d) == 0
        cos = jnp.dot(pick, jnp.cos(theta), precision=HIGHEST, preferred_element_type=jnp.float32)
        sin = jnp.dot(pick, jnp.sin(theta), precision=HIGHEST, preferred_element_type=jnp.float32)
        sin = jnp.where(low, -sin, sin)
        own.append([cos[16 * m : 16 * m + 16] for m in range(count)])
        other.append([sin[16 * m : 16 * m + 16] for m in range(count)])
        delays.append(d)

    def partner(values, d, m):
        result = values[m ^ 1]
        for k, g in enumerate(gens[1:], 1):
            result = jnp.where(d == g, values[m ^ (1 << k)], result)
        return result

    one = jnp.ones((16, 128), jnp.float32)
    zero = jnp.zeros((16, 128), jnp.float32)

    def row_of(start):
        values = [one if m == start else zero for m in range(count)]
        for section in (2, 1, 0):
            a, b, d = own[section], other[section], delays[section]
            scaled = [values[m] * b[m] for m in range(count)]
            values = [values[m] * a[m] + partner(scaled, d, m) for m in range(count)]
        return values

    def col_of():
        values = [one if m == 0 else zero for m in range(count)]
        for section in (0, 1, 2):
            a, b, d = own[section], other[section], delays[section]
            values = [values[m] * a[m] + b[m] * partner(values, d, m) for m in range(count)]
        return values

    for n, values in enumerate(
        (row_of(0), row_of(Plan.top_bit), col_of(), row_of(Plan.third_bit))
    ):
        for m in range(count):
            out[n, m] = values[m]


def coefficients(top, col_blocks, info, angles):
    return pl.pallas_call(
        functools.partial(coefficients_kernel, Plan.count, top, col_blocks),
        out_shape=jax.ShapeDtypeStruct((4, Plan.count, 16, 128), jnp.float32),
        in_specs=[SMEM, VMEM],
        out_specs=VMEM,
        compiler_params=pltpu.CompilerParams(vmem_limit_bytes=32 * 2**20),
    )(info, angles)


def row_kernel(plan, height, near_ref, top_ref, coef_ref, *outs, rows=slice(0, 8)):
    tables = [0, 3]
    blocks = height // 128
    far = plan.third_bit if plan.row_far else 0
    for which, out in enumerate(outs):
        table = tables[which]
        columns = [jnp.transpose(coef_ref[table, m, rows, :]) for m in range(plan.count)]
        for j in range(blocks):
            total = None
            for m in range(plan.count):
                if m & far:
                    continue
                ref = top_ref if m & plan.top_bit else near_ref
                value = plan.values[m] & ~plan.top
                i = j ^ value
                term = ref[128 * i : 128 * i + 128, :] * columns[m][:, j : j + 1]
                total = term if total is None else total + term
            out[128 * j : 128 * j + 128, :] = total


def mix_rows(plan, near, top, coef, width=128):
    height, all_width = near.shape
    n_out = 2 if plan.row_far else 1
    block = pl.BlockSpec((height, width), lambda i: (0, i))
    shape = jax.ShapeDtypeStruct(near.shape, jnp.float32)
    return pl.pallas_call(
        functools.partial(row_kernel, plan, height),
        grid=(all_width // width,),
        out_shape=[shape] * n_out,
        in_specs=[block, block, VMEM],
        out_specs=[block] * n_out,
        compiler_params=pltpu.CompilerParams(vmem_limit_bytes=48 * 2**20),
    )(near, top, coef)


def col_kernel(plan, *refs):
    if plan.col_far:
        near_ref, far_ref, coef_ref, mine, theirs = refs
    else:
        near_ref, coef_ref, mine, theirs = refs
        far_ref = None
    far = plan.third_bit if plan.col_far else 0
    for which, out in enumerate((mine, theirs)):
        for j in range(plan.col_blocks):
            total = None
            for m in range(plan.count):
                if m & plan.top_bit:
                    continue
                ref = far_ref if m & far else near_ref
                value = plan.values[m] & ~(plan.third if m & far else 0)
                i = j ^ value
                term = ref[:, 128 * i : 128 * i + 128] * coef_ref[which, m, 8 + j : 9 + j, :]
                total = term if total is None else total + term
            out[:, 128 * j : 128 * j + 128] = total


def mix_cols(plan, parts, coef, strip=128):
    height, width = parts[0].shape
    block = pl.BlockSpec((strip, width), lambda i: (i, 0))
    shape = jax.ShapeDtypeStruct((height, width), jnp.float32)
    return pl.pallas_call(
        functools.partial(col_kernel, plan),
        grid=(height // strip,),
        out_shape=[shape] * 2,
        in_specs=[block] * len(parts) + [VMEM],
        out_specs=[block] * 2,
        compiler_params=pltpu.CompilerParams(vmem_limit_bytes=48 * 2**20),
    )(*parts, coef)


def near_kernel(plan, height, near_ref, top_ref, coef_ref, mine, theirs, middle):
    blocks = height // 128
    start = pl.program_id(0) * blocks
    row_kernel(plan, height, near_ref, top_ref, coef_ref, middle, rows=pl.ds(start, blocks))
    col_kernel(plan, middle, coef_ref, mine, theirs)


def mix_near(plan, near, top, coef):
    height, width = near.shape
    half = height // 2
    block = pl.BlockSpec((half, width), lambda i: (i, 0))
    shape = jax.ShapeDtypeStruct((height, width), jnp.float32)
    return pl.pallas_call(
        functools.partial(near_kernel, plan, half),
        grid=(2,),
        out_shape=[shape] * 2,
        in_specs=[block, block, pl.BlockSpec(coef.shape[:2] + (16, 128), lambda i: (0, 0, 0, 0))],
        out_specs=[block] * 2,
        scratch_shapes=[pltpu.VMEM((half, width), jnp.float32)],
        compiler_params=pltpu.CompilerParams(vmem_limit_bytes=48 * 2**20),
    )(near, top, coef)


def dot(a, b, over=((1,), (0,))):
    return lax.dot_general(
        a, b, (over, ((), ())), precision=HIGHEST, preferred_element_type=jnp.float32
    )


def inverse_factor(block):
    n = block.shape[0]
    i = lax.broadcasted_iota(jnp.int32, (8, 2 * n), 0)
    lane = lax.broadcasted_iota(jnp.int32, (8, 2 * n), 1)
    unit = [jnp.where(lane == i + 8 * t + n, 1.0, 0.0) for t in range(n // 8)]
    wide = jnp.concatenate([block, jnp.zeros_like(block)], axis=1)
    tiles = [wide[8 * t : 8 * t + 8] + unit[t] for t in range(n // 8)]
    for j in range(n):
        first, r = divmod(j, 8)
        row = tiles[first][r : r + 1, :]
        scaled = row * (1.0 / row[:, j : j + 1])
        for t in range(first, n // 8):
            col = tiles[t][:, j : j + 1]
            if t == first:
                col = jnp.where(i[:, :1] > r, col, 0.0)
            tiles[t] = tiles[t] - col * scaled
    out = []
    for t in range(n // 8):
        pivot = jnp.sum(jnp.where(lane == i + 8 * t, tiles[t], 0.0), axis=1, keepdims=True)
        out.append(tiles[t][:, n:] * lax.rsqrt(pivot))
    return jnp.concatenate(out, axis=0)


def weights_kernel(square, given, out, work, right):
    size, n = square.shape[0], 64
    work[...] = square[...]
    right[...] = given[...]
    inverses = []
    for k in range(0, size, n):
        inverse = inverse_factor(work[k : k + n, k : k + n])
        inverses.append(inverse)
        mine = dot(inverse, right[k : k + n, :])
        right[k : k + n, :] = mine
        if k + n < size:
            below = dot(work[k + n :, k : k + n], inverse, ((1,), (1,)))
            work[k + n :, k : k + n] = below
            work[k + n :, k + n :] -= dot(below, below, ((1,), (1,)))
            right[k + n :, :] -= dot(below, mine)
    for k in range(size - n, -1, -n):
        rest = right[k : k + n, :]
        if k + n < size:
            rest = rest - dot(work[k + n :, k : k + n], out[k + n :, :], ((0,), (0,)))
        out[k : k + n, :] = dot(inverses[k // n], rest, ((0,), (0,)))


def solve_weights(square, given):
    return pl.pallas_call(
        weights_kernel,
        out_shape=jax.ShapeDtypeStruct(given.shape, jnp.float32),
        in_specs=[VMEM, VMEM],
        out_specs=VMEM,
        scratch_shapes=[
            pltpu.VMEM(square.shape, jnp.float32),
            pltpu.VMEM(given.shape, jnp.float32),
        ],
        compiler_params=pltpu.CompilerParams(vmem_limit_bytes=32 * 2**20),
    )(square, given)


def selection(coef, base, n_blocks, first, third, top, panel):
    n = n_blocks * QUANTUM
    ids = base * QUANTUM + jnp.arange(n, dtype=jnp.int32)
    slots = jnp.arange(2 * PANEL, dtype=jnp.int32)
    chosen = panel + jnp.where(slots < PANEL, slots, top * QUANTUM + slots - PANEL)
    result = jnp.zeros((2 * PANEL, n), jnp.float32)
    for m in range(Plan.count):
        at = ids ^ (((m & 1) + (m >> 1 & 1) * third + (m >> 2) * top) * QUANTUM)
        weight = coef[2, m, first : first + n_blocks].reshape(n)
        result = result + jnp.where(at[None, :] == chosen[:, None], weight[None, :], 0.0)
    return result


def gather_pairs(value):
    n_col = lax.axis_size("col")
    groups = [list(range(core, n_col, 2)) for core in (0, 1)]
    many = jnp.broadcast_to(value[None], (n_col // 2,) + value.shape)
    return lax.all_to_all(many, "col", 0, 0, axis_index_groups=groups)


def transposed(value):
    n_row, n_col = lax.axis_size("row"), lax.axis_size("col")
    pairs = []
    for r in range(n_row):
        for c in range(n_col):
            pairs.append((r * n_col + c, (c // 2) * n_col + r * 2 + c % 2))
    return lax.ppermute(value, ("row", "col"), pairs)


def mix_piece(plan, piece, top_piece, coef, third):
    moved = {0: piece, plan.top_bit: top_piece}
    far, far_value = plan.top_bit, plan.top
    if plan.col_far:
        pair = jnp.concatenate([piece, top_piece])
        pair = swap_far(pair, "col", third, plan.thirds, plan.col_blocks)
        moved[plan.third_bit] = pair[: piece.shape[0]]
        moved[plan.third_bit | plan.top_bit] = pair[piece.shape[0] :]
        far, far_value = far | plan.third_bit, far_value | plan.third
    mixed = []
    for j in range(plan.col_blocks):
        total = 0.0
        for m in range(plan.count):
            i = j ^ (plan.values[m] & ~far_value)
            source = moved[m & far][:, 128 * i : 128 * i + 128]
            total = total + source * coef[0, m, 8 + j][None, :]
        mixed.append(total)
    return jnp.concatenate(mixed, axis=1)


def mix_field(plan, covariance, over, coef, third):
    if not plan.col_far:
        return mix_near(plan, covariance, over, coef)
    if plan.row_far:
        mine, theirs = mix_rows(plan, covariance, over, coef)
        field = mine + swap_far(theirs, "row", third, plan.thirds, plan.row_blocks)
    else:
        (field,) = mix_rows(plan, covariance, over, coef)
    parts = [field, swap_far(field, "col", third, plan.thirds, plan.col_blocks)]
    return mix_cols(plan, parts, coef)


def shards(covariance, angles, delays, panel):
    rows_dev, cols_dev = covariance.shape
    n_row = lax.axis_size("row")
    row_blocks, col_blocks = rows_dev // QUANTUM, cols_dev // QUANTUM
    top = row_blocks * n_row // 2
    given = jnp.sum(delays) // QUANTUM - top - 1
    thirds = [1 << n for n in range(1, top.bit_length() - 1)]
    near = [t for t in thirds if t < min(row_blocks, col_blocks)]
    side = [t for t in thirds if col_blocks <= t < row_blocks]
    away = [t for t in thirds if t >= max(row_blocks, col_blocks)]
    plans = [Plan(group, top, row_blocks, col_blocks) for group in (near, side, away)]
    inner = (given > 1) & (given < top)
    third = jnp.where(inner, given, near[0])
    index = (third >= side[0]).astype(jnp.int32) + (third >= away[0]).astype(jnp.int32)
    rb = lax.axis_index("row").astype(jnp.int32) * row_blocks
    cb = lax.axis_index("col").astype(jnp.int32) * col_blocks
    info = jnp.concatenate([delays // QUANTUM, rb[None], cb[None], third[None]]).astype(jnp.int32)
    coef = coefficients(top, col_blocks, info, angles.reshape(3 * top, QUANTUM))

    sel_r = selection(coef, rb, row_blocks, 0, third, top, panel[0])
    sel_c = selection(coef, cb, col_blocks, 8, third, top, panel[0])
    part = jnp.dot(sel_r, covariance, precision=HIGHEST)
    covariance, part = lax.optimization_barrier((covariance, part))
    spread = lax.all_to_all(part.reshape(n_row, -1, cols_dev), "row", 0, 0)
    over = swap(covariance, "row", top // row_blocks)
    piece = jnp.sum(spread, axis=0)
    top_piece = swap(piece, "col", top // col_blocks)
    block = jnp.dot(piece, sel_c.T, precision=HIGHEST)
    block = block + swap(block, "col", 1)
    block = jnp.sum(gather_pairs(block), axis=0)
    over, block = lax.optimization_barrier((over, block))
    mixed = lax.switch(
        index, [functools.partial(mix_piece, plan) for plan in plans], piece, top_piece, coef, third
    )
    both = jnp.concatenate([mixed, block], axis=1)
    both = lax.all_to_all(jnp.broadcast_to(both[None], (n_row,) + both.shape), "row", 0, 0)
    mine, theirs = lax.switch(
        index, [functools.partial(mix_field, plan) for plan in plans], covariance, over, coef, third
    )
    theirs, both, mixed = lax.optimization_barrier((theirs, both, mixed))

    both = both.reshape(2 * PANEL, -1)
    rows_part, square = both[:, :cols_dev], both[:, cols_dev:]
    arrived = swap(theirs, "col", top // col_blocks)
    weights = solve_weights(square, rows_part)
    here = gather_pairs(transposed(mixed)).reshape(2 * PANEL, cols_dev)
    here, weights = lax.optimization_barrier((here, weights))
    twin = swap(here, "col", 1)
    low = lax.axis_index("col") % 2 == 0
    columns = jnp.concatenate([jnp.where(low, here, twin), jnp.where(low, twin, here)], axis=1)
    update = lax.dot_general(columns, weights, (((0,), (0,)), ((), ())), precision=HIGHEST)
    return mine + arrived - update


def solution(mesh):
    in_specs = (P("row", "col"), P(), P(), P())
    out_specs = P("row", "col")
    return jax.shard_map(shards, mesh=mesh, in_specs=in_specs, out_specs=out_specs, check_vma=False)
```

time: 505 us -> 352 us (0.70)
  the two profiles are of different devices: /device:TPU:23 before, /device:TPU:40 now
where the time goes in v1:
time: 352 us; the launch traced here: 351 us
  waiting for transfers between devices  205 us (58%)
  starting transfers between devices  92.4 us (26%)
  Pallas kernels  32.7 us (9%)
  matrix products  11.7 us (3%)
  local copies, waits for them, and re-layouts  3.66 us (1%)
  between operations  3.55 us (1%)
    ppermute x5, waiting for transfers between devices, swap(): return lax.ppermute(value, axis, pairs)  182 us
    all_to_all x2, starting transfers between devices, gather_pairs(): return lax.all_to_all(many, 'col', 0, 0, axis_index_groups=groups)  45.2 us
    ppermute x5, starting transfers between devices, swap(): return lax.ppermute(value, axis, pairs)  32.9 us
    pallas_call x1, Pallas kernels, solve_weights(): pl.pallas_call(weights_kernel, out_shape=jax.ShapeDtypeStruct(given.shape...  26 us
    all_to_all x1, waiting for transfers between devices, shards(): lax.all_to_all(jnp.broadcast_to(both[None], (n_row,) + both.shape), 'row'...  13 us
    all_to_all x1, waiting for transfers between devices, shards(): spread = lax.all_to_all(part.reshape(n_row, -1, cols_dev), 'row', 0, 0)  9.41 us
    all_to_all x1, starting transfers between devices, shards(): spread = lax.all_to_all(part.reshape(n_row, -1, cols_dev), 'row', 0, 0)  8.49 us
  transfers between devices with their start and end apart: 10, of which 7 were waited for; matrix products, arithmetic and copies ran while one was open for 1% of the time, Pallas kernels for 9%

profile of v1, /device:TPU:40, one launch (start us, length us, event | category | flops | bytes accessed | tf_op | source)
XLA Modules:
  0.0 351.0 jit_solution(4527833841509951981)
XLA Ops:
  0.0 1.3 and_select_fusion
  3.9 1.0 reshape.186.angles
  4.9 0.1 pad_add_fusion.info
  5.0 1.4 shard_map.46
  7.2 5.3 %fusion.6 = f32[256,512]{1,0:T(8,128)} fusion(f32[1024,512]{1,0:T(8,128)} %param.19, f32[1024]{0:T(1024)S(1)} %get-tuple-element.239, s32[1024]{0:T(1024)S(1)} %get-tuple-element.249, f32[1024]{0:T(1024)S(1)} %get-tuple-element.240, s32[1024]{0:T(1024)S(1)} %get-tuple-element.250, f32[1024]{0:T(1024)S(1)} %get-tuple-element.241, ...), kind=kOutput, calls=%fused_computation.118 | convolution fusion | flops 1616642048 | bytes 2688000 | tf_op jit(solution)/shard_map/dot_general | solution.py:349
  12.4 8.5 %all-to-all-start = ((f32[16,16,512]{2,1,0:T(8,128)}), f32[16,16,512]{2,1,0:T(8,128)S(1)}, u32[]{:S(2)}, u32[]{:S(2)}) async-start(f32[16,16,512]{2,1,0:T(8,128)} %bitcast.108), calls=%async_computation | async-start | bytes 1048576 | tf_op jit(solution)/shard_map/all_to_all | solution.py:351
  20.9 4.9 %collective-permute-start.11 = (f32[1024,512]{1,0:T(8,128)S(1)}, f32[1024,512]{1,0:T(8,128)}, u32[]{:S(2)}, u32[]{:S(2)}) collective-permute-start(f32[1024,512]{1,0:T(8,128)S(1)} %copy-done), channel_id=1, source_target_pairs={{0,256},{32,288},{64,320},{96,352},{128,384},{160,416},{192,448},{... | collective-permute-start | bytes 6291464 | tf_op jit(solution)/shard_map/ppermute | solution.py:19
  25.9 9.4 %all-to-all-done = f32[16,16,512]{2,1,0:T(8,128)S(1)} async-done(((f32[16,16,512]{2,1,0:T(8,128)}), f32[16,16,512]{2,1,0:T(8,128)S(1)}, u32[]{:S(2)}, u32[]{:S(2)}) %all-to-all-start) | async-done | bytes 524320 | tf_op jit(solution)/shard_map/all_to_all | solution.py:351
  35.3 0.9 fusion.30
  36.2 1.9 collective-permute-start.12
  38.2 1.1 collective-permute-done.12
  39.3 0.7 broadcast_in_dim.236
  40.0 15.5 %all-to-all-start.1 = ((f32[16,16,256]{2,1,0:T(8,128)}), f32[16,16,256]{2,1,0:T(8,128)S(1)}, u32[]{:S(2)}, u32[]{:S(2)}) async-start(f32[16,16,256]{2,1,0:T(8,128)} %broadcast_in_dim.236), calls=%async_computation.1 | async-start | bytes 524288 | tf_op jit(solution)/shard_map/all_to_all | solution.py:284
  55.5 12.1 %collective-permute-start.13 = (f32[16,512]{1,0:T(8,128)S(1)}, f32[16,512]{1,0:T(8,128)S(1)}, u32[]{:S(2)}, u32[]{:S(2)}) collective-permute-start(f32[16,512]{1,0:T(8,128)S(1)} %reduce_sum.28), channel_id=1, source_target_pairs={{0,16},{1,17},{2,18},{3,19},{4,20},{5,21},{6,22},{7,23},{8,24},{9,... | collective-permute-start | bytes 98312 | tf_op jit(solution)/shard_map/ppermute | solution.py:19
  67.6 12.1 %collective-permute-done.13 = f32[16,512]{1,0:T(8,128)S(1)} collective-permute-done((f32[16,512]{1,0:T(8,128)S(1)}, f32[16,512]{1,0:T(8,128)S(1)}, u32[]{:S(2)}, u32[]{:S(2)}) %collective-permute-start.13) | collective-permute-done | bytes 32800 | tf_op jit(solution)/shard_map/ppermute | solution.py:19
  79.7 0.1 conditional.6
  79.9 1.0 broadcast_in_dim.237
  80.8 5.1 %all-to-all-start.2 = ((f32[16,16,768]{2,1,0:T(8,128)}), f32[16,16,768]{2,1,0:T(8,128)S(1)}, u32[]{:S(2)}, u32[]{:S(2)}) async-start(f32[16,16,768]{2,1,0:T(8,128)} %broadcast_in_dim.237), calls=%async_computation.2 | async-start | bytes 1572864 | tf_op jit(solution)/shard_map/all_to_all | solution.py:363
  85.9 5.3 %conditional.5 = ((f32[1024,512]{1,0:T(8,128)}, f32[1024,512]{1,0:T(8,128)})) conditional(s32[]{:T(128)} %clamp.11, (f32[1024,512]{1,0:T(8,128)S(1)}, f32[1024,512]{1,0:T(8,128)}, f32[4,8,16,128]{3,2,1,0:T(8,128)S(1)}) %tuple.208, (f32[1024,512]{1,0:T(8,128)S(1)}, f32[1024,512]{1,0:T(8,128)}, ...), branch_computations={%region_3.4_spmd, %region_4.5_spmd, %region_5.12_spmd} | conditional | flops 524294 | bytes 39846104 | solution.py:364
  85.9 5.3 %branch_0_fun.1 = (f32[1024,512]{1,0:T(8,128)}, f32[1024,512]{1,0:T(8,128)}) custom-call(f32[1024,512]{1,0:T(8,128)S(1)} %get-tuple-element.88.near_ref, f32[1024,512]{1,0:T(8,128)} %get-tuple-element.89.top_ref, f32[4,8,16,128]{3,2,1,0:T(8,128)S(1)} %get-tuple-element.90.coef_ref), custom_call_target="tpu_custom_call" | custom-call | tf_op jit(solution)/shard_map/cond/branch_0_fun/pallas_call | solution.py:191
  91.3 13.0 %all-to-all-done.2 = f32[16,16,768]{2,1,0:T(8,128)S(1)} async-done(((f32[16,16,768]{2,1,0:T(8,128)}), f32[16,16,768]{2,1,0:T(8,128)S(1)}, u32[]{:S(2)}, u32[]{:S(2)}) %all-to-all-start.2) | async-done | bytes 786464 | tf_op jit(solution)/shard_map/all_to_all | solution.py:363
  104.3 0.8 collective-permute-start.15
  105.1 0.9 broadcast_in_dim.238
  106.0 29.7 %all-to-all-start.3 = ((f32[16,16,512]{2,1,0:T(8,128)}), f32[16,16,512]{2,1,0:T(8,128)S(1)}, u32[]{:S(2)}, u32[]{:S(2)}) async-start(f32[16,16,512]{2,1,0:T(8,128)} %broadcast_in_dim.238), calls=%async_computation.3 | async-start | bytes 1048576 | tf_op jit(solution)/shard_map/all_to_all | solution.py:284
  135.7 12.1 %collective-permute-start.14 = (f32[1024,512]{1,0:T(8,128)}, f32[1024,512]{1,0:T(8,128)}, u32[]{:S(2)}, u32[]{:S(2)}) collective-permute-start(f32[1024,512]{1,0:T(8,128)} %get-tuple-element.127), channel_id=1, source_target_pairs={{0,16},{1,17},{2,18},{3,19},{4,20},{5,21},{6,22},{7,23},{8,24},{9,... | collective-permute-start | bytes 6291464 | tf_op jit(solution)/shard_map/ppermute | solution.py:19
  147.8 26.0 %shard_map.47 = f32[256,512]{1,0:T(8,128)S(1)} custom-call(f32[256,256]{1,0:T(8,128)S(1)} %slice.652.square, f32[256,512]{1,0:T(8,128)S(1)} %slice.653.given), custom_call_target="tpu_custom_call" | custom-call | tf_op jit(solution)/shard_map/pallas_call | solution.py:254
  173.9 0.6 all-to-all-done.3
  174.4 1.9 collective-permute-start.16
  176.4 1.9 collective-permute-done.16
  178.2 0.1 broadcast_select_fusion.1
  178.3 167.2 %collective-permute-done.14 = f32[1024,512]{1,0:T(8,128)} collective-permute-done((f32[1024,512]{1,0:T(8,128)}, f32[1024,512]{1,0:T(8,128)}, u32[]{:S(2)}, u32[]{:S(2)}) %collective-permute-start.14) | collective-permute-done | bytes 2097184 | tf_op jit(solution)/shard_map/ppermute | solution.py:19
  345.5 5.5 %add_subtract_fusion = f32[1024,512]{1,0:T(8,128)} fusion(f32[1024,512]{1,0:T(8,128)} %get-tuple-element.124, f32[1024,512]{1,0:T(8,128)} %collective-permute-done.14, f32[256,512]{1,0:T(8,128)S(1)} %shard_map.47, f32[256,512]{1,0:T(8,128)S(1)} %get-tuple-element.229, f32[256,512]{1,0:T(8,128)S(1)} %get-tuple-element.228), kind=kOutput, calls=%fused_computation.113 | convolution fusion | flops 1611923456 | bytes 7864320 | tf_op jit(solution)/shard_map/dot_general | solution.py:378
  (29 shorter events, 0.3 us)
Async XLA Ops:
  7.1 13.8 %copy-start = (f32[1024,512]{1,0:T(8,128)S(1)}, f32[1024,512]{1,0:T(8,128)}, u32[]{:S(2)}) copy-start(f32[1024,512]{1,0:T(8,128)} %param.19) | copy-start | bytes 6291460
  12.4 22.9 %all-to-all-start = ((f32[16,16,512]{2,1,0:T(8,128)}), f32[16,16,512]{2,1,0:T(8,128)S(1)}, u32[]{:S(2)}, u32[]{:S(2)}) async-start(f32[16,16,512]{2,1,0:T(8,128)} %bitcast.108), calls=%async_computation | async-start | bytes 1048576 | tf_op jit(solution)/shard_map/all_to_all | solution.py:351
  20.9 59.0 %collective-permute-start.11 = (f32[1024,512]{1,0:T(8,128)S(1)}, f32[1024,512]{1,0:T(8,128)}, u32[]{:S(2)}, u32[]{:S(2)}) collective-permute-start(f32[1024,512]{1,0:T(8,128)S(1)} %copy-done), channel_id=1, source_target_pairs={{0,256},{32,288},{64,320},{96,352},{128,384},{160,416},{192,448},{... | collective-permute-start | bytes 6291464 | tf_op jit(solution)/shard_map/ppermute | solution.py:19
  36.2 3.1 collective-permute-start.12
  40.0 39.8 %all-to-all-start.1 = ((f32[16,16,256]{2,1,0:T(8,128)}), f32[16,16,256]{2,1,0:T(8,128)S(1)}, u32[]{:S(2)}, u32[]{:S(2)}) async-start(f32[16,16,256]{2,1,0:T(8,128)} %broadcast_in_dim.236), calls=%async_computation.1 | async-start | bytes 524288 | tf_op jit(solution)/shard_map/all_to_all | solution.py:284
  55.5 24.2 %collective-permute-start.13 = (f32[16,512]{1,0:T(8,128)S(1)}, f32[16,512]{1,0:T(8,128)S(1)}, u32[]{:S(2)}, u32[]{:S(2)}) collective-permute-start(f32[16,512]{1,0:T(8,128)S(1)} %reduce_sum.28), channel_id=1, source_target_pairs={{0,16},{1,17},{2,18},{3,19},{4,20},{5,21},{6,22},{7,23},{8,24},{9,... | collective-permute-start | bytes 98312 | tf_op jit(solution)/shard_map/ppermute | solution.py:19
  80.8 23.4 %all-to-all-start.2 = ((f32[16,16,768]{2,1,0:T(8,128)}), f32[16,16,768]{2,1,0:T(8,128)S(1)}, u32[]{:S(2)}, u32[]{:S(2)}) async-start(f32[16,16,768]{2,1,0:T(8,128)} %broadcast_in_dim.237), calls=%async_computation.2 | async-start | bytes 1572864 | tf_op jit(solution)/shard_map/all_to_all | solution.py:363
  104.3 0.8 collective-permute-start.15
  106.0 68.5 %all-to-all-start.3 = ((f32[16,16,512]{2,1,0:T(8,128)}), f32[16,16,512]{2,1,0:T(8,128)S(1)}, u32[]{:S(2)}, u32[]{:S(2)}) async-start(f32[16,16,512]{2,1,0:T(8,128)} %broadcast_in_dim.238), calls=%async_computation.3 | async-start | bytes 1048576 | tf_op jit(solution)/shard_map/all_to_all | solution.py:284
  135.7 209.8 %collective-permute-start.14 = (f32[1024,512]{1,0:T(8,128)}, f32[1024,512]{1,0:T(8,128)}, u32[]{:S(2)}, u32[]{:S(2)}) collective-permute-start(f32[1024,512]{1,0:T(8,128)} %get-tuple-element.127), channel_id=1, source_target_pairs={{0,16},{1,17},{2,18},{3,19},{4,20},{5,21},{6,22},{7,23},{8,24},{9,... | collective-permute-start | bytes 6291464 | tf_op jit(solution)/shard_map/ppermute | solution.py:19
  174.4 3.8 %collective-permute-start.16 = (f32[256,512]{1,0:T(8,128)S(1)}, f32[256,512]{1,0:T(8,128)S(1)}, u32[]{:S(2)}, u32[]{:S(2)}) collective-permute-start(f32[256,512]{1,0:T(8,128)S(1)} %bitcast.237), channel_id=1, source_target_pairs={{0,1},{1,0},{2,3},{3,2},{4,5},{5,4},{6,7},{7,6},{8,9},{9,8},{10,11... | collective-permute-start | bytes 1572872 | tf_op jit(solution)/shard_map/ppermute | solution.py:19

commit v2 on v1

--- a/solution.py
+++ b/solution.py
@@ -8,6 +8,7 @@
 from jax.sharding import PartitionSpec as P
 
 PANEL = 128
+X, Y, Z_LO, Z_HI = 4, 4, 4, 4
 QUANTUM = 128
 HIGHEST = lax.Precision.HIGHEST
 VMEM = pl.BlockSpec(memory_space=pltpu.VMEM)
@@ -17,6 +18,17 @@
 def swap(value, axis, mask):
     pairs = [(source, source ^ mask) for source in range(lax.axis_size(axis))]
     return lax.ppermute(value, axis, pairs)
+
+
+def gather(value, axis, stride, count):
+    size = lax.axis_size(axis)
+    groups = [
+        [low + stride * k + high for k in range(count)]
+        for high in range(0, size, stride * count)
+        for low in range(stride)
+    ]
+    many = jnp.broadcast_to(value[None], (count,) + value.shape)
+    return lax.all_to_all(many, axis, 0, 0, axis_index_groups=groups)
 
 
 def swap_far(value, axis, third, thirds, per_device):
@@ -176,25 +188,24 @@
     )(*parts, coef)
 
 
-def near_kernel(plan, height, near_ref, top_ref, coef_ref, mine, theirs, middle):
-    blocks = height // 128
-    start = pl.program_id(0) * blocks
-    row_kernel(plan, height, near_ref, top_ref, coef_ref, middle, rows=pl.ds(start, blocks))
+def near_kernel(plan, near_ref, top_ref, coef_ref, mine, theirs, middle):
+    blocks = near_ref.shape[0] // QUANTUM
+    rows = pl.ds(pl.program_id(0) * blocks, blocks)
+    row_kernel(plan, near_ref.shape[0], near_ref, top_ref, coef_ref, middle, rows=rows)
     col_kernel(plan, middle, coef_ref, mine, theirs)
 
 
 def mix_near(plan, near, top, coef):
     height, width = near.shape
-    half = height // 2
-    block = pl.BlockSpec((half, width), lambda i: (i, 0))
+    block = pl.BlockSpec((height // 2, width), lambda i: (i, 0))
     shape = jax.ShapeDtypeStruct((height, width), jnp.float32)
     return pl.pallas_call(
-        functools.partial(near_kernel, plan, half),
+        functools.partial(near_kernel, plan),
         grid=(2,),
         out_shape=[shape] * 2,
-        in_specs=[block, block, pl.BlockSpec(coef.shape[:2] + (16, 128), lambda i: (0, 0, 0, 0))],
+        in_specs=[block, block, pl.BlockSpec(coef.shape, lambda i: (0, 0, 0, 0))],
         out_specs=[block] * 2,
-        scratch_shapes=[pltpu.VMEM((half, width), jnp.float32)],
+        scratch_shapes=[pltpu.VMEM((height // 2, width), jnp.float32)],
         compiler_params=pltpu.CompilerParams(vmem_limit_bytes=48 * 2**20),
     )(near, top, coef)
 
@@ -277,19 +288,16 @@
     return result
 
 
-def gather_pairs(value):
-    n_col = lax.axis_size("col")
-    groups = [list(range(core, n_col, 2)) for core in (0, 1)]
-    many = jnp.broadcast_to(value[None], (n_col // 2,) + value.shape)
-    return lax.all_to_all(many, "col", 0, 0, axis_index_groups=groups)
-
-
 def transposed(value):
     n_row, n_col = lax.axis_size("row"), lax.axis_size("col")
+    cores = n_col // (Z_HI * Y)
     pairs = []
     for r in range(n_row):
+        x, z_lo = divmod(r, Z_LO)
         for c in range(n_col):
-            pairs.append((r * n_col + c, (c // 2) * n_col + r * 2 + c % 2))
+            z_hi, y, core = c // cores // Y, c // cores % Y, c % cores
+            to = (z_hi * Z_LO + y) * n_col + (z_lo * Y + x) * cores + core
+            pairs.append((r * n_col + c, to))
     return lax.ppermute(value, ("row", "col"), pairs)
 
 
@@ -347,36 +355,52 @@
     sel_r = selection(coef, rb, row_blocks, 0, third, top, panel[0])
     sel_c = selection(coef, cb, col_blocks, 8, third, top, panel[0])
     part = jnp.dot(sel_r, covariance, precision=HIGHEST)
-    covariance, part = lax.optimization_barrier((covariance, part))
     spread = lax.all_to_all(part.reshape(n_row, -1, cols_dev), "row", 0, 0)
     over = swap(covariance, "row", top // row_blocks)
     piece = jnp.sum(spread, axis=0)
-    top_piece = swap(piece, "col", top // col_blocks)
     block = jnp.dot(piece, sel_c.T, precision=HIGHEST)
-    block = block + swap(block, "col", 1)
-    block = jnp.sum(gather_pairs(block), axis=0)
-    over, block = lax.optimization_barrier((over, block))
+    cores = lax.axis_size("col") // (Z_HI * Y)
+    along = gather(jnp.concatenate([piece, block], axis=1), "col", cores * Y, Z_HI)
+    z_hi = lax.axis_index("col") // (cores * Y)
+    apart = top // col_blocks // (cores * Y)
+    top_piece = lax.dynamic_index_in_dim(along, z_hi ^ apart, 0, keepdims=False)[:, :cols_dev]
+    block = jnp.sum(along[:, :, cols_dev:], axis=0)
     mixed = lax.switch(
         index, [functools.partial(mix_piece, plan) for plan in plans], piece, top_piece, coef, third
     )
-    both = jnp.concatenate([mixed, block], axis=1)
-    both = lax.all_to_all(jnp.broadcast_to(both[None], (n_row,) + both.shape), "row", 0, 0)
-    mine, theirs = lax.switch(
-        index, [functools.partial(mix_field, plan) for plan in plans], covariance, over, coef, third
+    quarter = gather(jnp.concatenate([mixed, block], axis=1), "row", 1, Z_LO)
+    over, quarter = lax.optimization_barrier((over, quarter))
+    quarter = quarter.reshape(-1, cols_dev + 2 * PANEL)
+    flipped = transposed(quarter[:, :cols_dev])
+    mine, moving = lax.switch(
+        index,
+        [functools.partial(mix_field, plan) for plan in plans],
+        covariance, over, coef, third,
     )
-    theirs, both, mixed = lax.optimization_barrier((theirs, both, mixed))
-
-    both = both.reshape(2 * PANEL, -1)
-    rows_part, square = both[:, :cols_dev], both[:, cols_dev:]
-    arrived = swap(theirs, "col", top // col_blocks)
-    weights = solve_weights(square, rows_part)
-    here = gather_pairs(transposed(mixed)).reshape(2 * PANEL, cols_dev)
-    here, weights = lax.optimization_barrier((here, weights))
-    twin = swap(here, "col", 1)
-    low = lax.axis_index("col") % 2 == 0
-    columns = jnp.concatenate([jnp.where(low, here, twin), jnp.where(low, twin, here)], axis=1)
-    update = lax.dot_general(columns, weights, (((0,), (0,)), ((), ())), precision=HIGHEST)
-    return mine + arrived - update
+    moving, quarter, flipped = lax.optimization_barrier((moving, quarter, flipped))
+
+    arrived = swap(moving, "col", top // col_blocks)
+
+    def finish(quarter, flipped, mine):
+        pieces = jnp.concatenate([quarter[:, cols_dev:], flipped], axis=1)
+        pieces = gather(pieces, "col", cores, Y)
+        block = jnp.sum(pieces[:, :, : 2 * PANEL], axis=0)
+        block = block + swap(block, "col", 1)
+        here = pieces[:, :, 2 * PANEL :].reshape(2 * PANEL, cols_dev)
+        twin = swap(here, "col", 1)
+        both = gather(jnp.concatenate([quarter[:, :cols_dev], block], axis=1), "row", Z_LO, X)
+        both = both.reshape(2 * PANEL, -1)
+        weights = solve_weights(both[:, cols_dev:], both[:, :cols_dev])
+        low = lax.axis_index("col") % 2 == 0
+        columns = jnp.concatenate([jnp.where(low, here, twin), jnp.where(low, twin, here)], axis=1)
+        update = lax.dot_general(columns, weights, (((0,), (0,)), ((), ())), precision=HIGHEST)
+        return mine - update
+
+    rest = lax.cond(
+        panel[0] >= 0, finish, lambda quarter, flipped, mine: mine,
+        quarter, flipped, mine,
+    )
+    return rest + arrived
 
 
 def solution(mesh):

time: 352 us -> 452 us (1.28)
  the two profiles are of different devices: /device:TPU:40 before, /device:TPU:103 now
where the time goes in v2:
time: 452 us; the launch traced here: 451 us
  waiting for transfers between devices  292 us (65%)
  starting transfers between devices  64.9 us (14%)
  Pallas kernels  41.2 us (9%)
  blocking collectives  15.2 us (3%)
  other arithmetic  11.9 us (3%)
  local copies, waits for them, and re-layouts  10.9 us (2%)
  matrix products  10.9 us (2%)
    ppermute x7, waiting for transfers between devices, swap(): return lax.ppermute(value, axis, pairs)  257 us
    ppermute x7, starting transfers between devices, swap(): return lax.ppermute(value, axis, pairs)  27.9 us
    pallas_call x1, Pallas kernels, solve_weights(): pl.pallas_call(weights_kernel, out_shape=jax.ShapeDtypeStruct(given.shape...  26 us
    all_to_all x3, waiting for transfers between devices, gather(): return lax.all_to_all(many, axis, 0, 0, axis_index_groups=groups)  25.2 us
    all_to_all x3, starting transfers between devices, gather(): return lax.all_to_all(many, axis, 0, 0, axis_index_groups=groups)  21 us
    all_to_all x1, blocking collectives, gather(): return lax.all_to_all(many, axis, 0, 0, axis_index_groups=groups)  15.2 us
    all_to_all x1, waiting for transfers between devices, shards(): spread = lax.all_to_all(part.reshape(n_row, -1, cols_dev), 'row', 0, 0)  9.39 us
    ppermute x1, starting transfers between devices, transposed(): return lax.ppermute(value, ('row', 'col'), pairs)  9.04 us
  transfers between devices with their start and end apart: 12, of which 9 were waited for; matrix products, arithmetic and copies ran while one was open for 4% of the time, Pallas kernels for 9%

profile of v2, /device:TPU:103, one launch (start us, length us, event | category | flops | bytes accessed | tf_op | source)
XLA Modules:
  0.0 450.9 jit_solution(3790494611895737824)
XLA Ops:
  7.2 5.3 %fusion.4 = f32[256,512]{1,0:T(8,128)} fusion(f32[1024,512]{1,0:T(8,128)} %param.21, f32[1024]{0:T(1024)S(1)} %get-tuple-element.261, s32[1024]{0:T(1024)S(1)} %get-tuple-element.271, f32[1024]{0:T(1024)S(1)} %get-tuple-element.262, s32[1024]{0:T(1024)S(1)} %get-tuple-element.272, f32[1024]{0:T(1024)S(1)} %get-tuple-element.263, ...), kind=kOutput, calls=%fused_computation.123 | convolution fusion | flops 1616642048 | bytes 2688000 | tf_op jit(solution)/shard_map/dot_general | solution.py:357
  12.4 6.9 %all-to-all-start.2 = ((f32[16,16,512]{2,1,0:T(8,128)}), f32[16,16,512]{2,1,0:T(8,128)S(1)}, u32[]{:S(2)}, u32[]{:S(2)}) async-start(f32[16,16,512]{2,1,0:T(8,128)} %bitcast.110), calls=%async_computation.2 | async-start | bytes 1048576 | tf_op jit(solution)/shard_map/all_to_all | solution.py:358
  19.4 3.1 collective-permute-start.13
  22.5 9.4 %all-to-all-done.2 = f32[16,16,512]{2,1,0:T(8,128)S(1)} async-done(((f32[16,16,512]{2,1,0:T(8,128)}), f32[16,16,512]{2,1,0:T(8,128)S(1)}, u32[]{:S(2)}, u32[]{:S(2)}) %all-to-all-start.2) | async-done | bytes 524320 | tf_op jit(solution)/shard_map/all_to_all | solution.py:358
  33.6 12.2 %all-to-all-start.3 = ((f32[4,16,768]{2,1,0:T(8,128)}), f32[4,16,768]{2,1,0:T(8,128)S(1)}, u32[]{:S(2)}, u32[]{:S(2)}) async-start(f32[4,16,768]{2,1,0:T(8,128)} %broadcast_in_dim.242), calls=%async_computation.3 | async-start | bytes 393216 | tf_op jit(solution)/shard_map/all_to_all | solution.py:31
  45.8 12.6 %all-to-all-done.3 = f32[4,16,768]{2,1,0:T(8,128)S(1)} async-done(((f32[4,16,768]{2,1,0:T(8,128)}), f32[4,16,768]{2,1,0:T(8,128)S(1)}, u32[]{:S(2)}, u32[]{:S(2)}) %all-to-all-start.3) | async-done | bytes 196640 | tf_op jit(solution)/shard_map/all_to_all | solution.py:31
  58.4 10.1 %conditional.6 = (f32[16,512]{1,0:T(8,128)S(1)}) conditional(s32[]{:T(128)} %clamp.11, (f32[16,512]{1,0:T(8,128)S(1)}, f32[4,8,16,128]{3,2,1,0:T(8,128)S(1)}, f32[16,512]{1,0:T(8,128)S(1)}) %tuple.86, (f32[16,512]{1,0:T(8,128)S(1)}, f32[4,8,16,128]{3,2,1,0:T(8,128)S(1)}, f32[16,512]{1,0:T(8,128)S(1)}) %tuple.86, ...), branch_computations={%region_2.3_spmd, %region_3.4_spmd, %region_4.8_spmd} | conditional | flops 163846 | bytes 802928 | solution.py:368
  58.5 6.9 %conditional = (f32[32,512]{1,0:T(8,128)}) conditional(s32[]{:T(128)} %clamp.1, f32[32,512]{1,0:T(8,128)S(1)} %pad_maximum_fusion.3, f32[32,512]{1,0:T(8,128)S(1)} %pad_maximum_fusion.3, f32[32,512]{1,0:T(8,128)S(1)} %pad_maximum_fusion.3), branch_computations={%region_5.5_spmd, %region_6.6_spmd, %region_7.7_spmd} | conditional | bytes 262192 | solution.py:39
  58.5 4.8 %collective-permute-start.1 = (f32[32,512]{1,0:T(8,128)S(1)}, f32[32,512]{1,0:T(8,128)}, u32[]{:S(2)}, u32[]{:S(2)}) collective-permute-start(f32[32,512]{1,0:T(8,128)S(1)} %param.3), channel_id=1, source_target_pairs={{0,4},{1,5},{2,6},{3,7},{4,0},{5,1},{6,2},{7,3},{8,12},{9,13},{10,... | collective-permute-start | bytes 196616 | tf_op jit(solution)/shard_map/cond/branch_2_fun/cond/branch_1_fun/ppermute | solution.py:20
  69.2 4.9 %all-to-all-start.4 = ((f32[4,16,768]{2,1,0:T(8,128)}), f32[4,16,768]{2,1,0:T(8,128)S(1)}, u32[]{:S(2)}, u32[]{:S(2)}) async-start(f32[4,16,768]{2,1,0:T(8,128)} %broadcast_in_dim.243), calls=%async_computation.4 | async-start | bytes 393216 | tf_op jit(solution)/shard_map/all_to_all | solution.py:31
  74.1 3.5 all-to-all-done.4
  77.7 9.0 %collective-permute-start.14 = (f32[64,512]{1,0:T(8,128)S(1)}, f32[64,512]{1,0:T(8,128)S(1)}, u32[]{:S(2)}, u32[]{:S(2)}) collective-permute-start(f32[64,512]{1,0:T(8,128)S(1)} %slice.680), channel_id=1, source_target_pairs={{0,0},{1,1},{2,32},{3,33},{4,64},{5,65},{6,96},{7,97},{8,128},{9,1... | collective-permute-start | bytes 393224 | tf_op jit(solution)/shard_map/ppermute | solution.py:301
  86.7 166.6 %conditional.7 = (f32[1024,512]{1,0:T(8,128)}, f32[1024,512]{1,0:T(8,128)}, f32[1024,512]{1,0:T(8,128)S(1)}, f32[1024,512]{1,0:T(8,128)}) conditional(s32[]{:T(128)} %clamp.11, (f32[1024,512]{1,0:T(8,128)S(1)}, f32[1024,512]{1,0:T(8,128)}, f32[4,8,16,128]{3,2,1,0:T(8,128)S(1)}) %tuple.230, (f32[1024,512]{1,0:T(8,128)S(1)}, ...), branch_computations={%region_9.10_spmd, %region_10.11_spmd, %region_11.18_spmd} | conditional | flops 524294 | bytes 48234736 | solution.py:375
  88.1 7.1 %branch_2_fun.2 = (f32[1024,512]{1,0:T(8,128)S(1)}, f32[1024,512]{1,0:T(8,128)S(1)}) custom-call(f32[1024,512]{1,0:T(8,128)} %copy-done.1, f32[1024,512]{1,0:T(8,128)} %get-tuple-element.130.top_ref, f32[4,8,16,128]{3,2,1,0:T(8,128)S(1)} %get-tuple-element.131.coef_ref.refs_2_), custom_call_target="tpu_custom_call" | custom-call | tf_op jit(solution)/shard_map/cond/branch_2_fun/pallas_call | solution.py:146
  95.2 94.3 %conditional.1 = (f32[1024,512]{1,0:T(8,128)}) conditional(s32[]{:T(128)} %clamp.3, f32[1024,512]{1,0:T(8,128)S(1)} %get-tuple-element.134, f32[1024,512]{1,0:T(8,128)S(1)} %get-tuple-element.134, f32[1024,512]{1,0:T(8,128)S(1)} %get-tuple-element.134), branch_computations={%region_12.12_spmd, %region_13.13_spmd, %region_14.14_spmd} | conditional | bytes 8388656 | solution.py:39
  95.2 3.7 collective-permute-start.5
  98.9 90.6 %collective-permute-done.5 = f32[1024,512]{1,0:T(8,128)} collective-permute-done((f32[1024,512]{1,0:T(8,128)S(1)}, f32[1024,512]{1,0:T(8,128)}, u32[]{:S(2)}, u32[]{:S(2)}) %collective-permute-start.5) | collective-permute-done | bytes 2097184 | tf_op jit(solution)/shard_map/cond/branch_2_fun/cond/branch_1_fun/ppermute | solution.py:20
  192.9 49.0 %conditional.2 = (f32[1024,512]{1,0:T(8,128)}) conditional(s32[]{:T(128)} %clamp.3, f32[1024,512]{1,0:T(8,128)S(1)} %add.408.refs_0_, f32[1024,512]{1,0:T(8,128)S(1)} %add.408.refs_0_, f32[1024,512]{1,0:T(8,128)S(1)} %add.408.refs_0_), branch_computations={%region_15.15_spmd, %region_16.16_spmd, %region_17.17_spmd} | conditional | bytes 8388656 | solution.py:39
  192.9 2.5 collective-permute-start.8
  195.4 46.5 %collective-permute-done.8 = f32[1024,512]{1,0:T(8,128)} collective-permute-done((f32[1024,512]{1,0:T(8,128)S(1)}, f32[1024,512]{1,0:T(8,128)}, u32[]{:S(2)}, u32[]{:S(2)}) %collective-permute-start.8) | collective-permute-done | bytes 2097184 | tf_op jit(solution)/shard_map/cond/branch_2_fun/cond/branch_1_fun/ppermute | solution.py:20
  241.9 6.7 %branch_2_fun.3 = (f32[1024,512]{1,0:T(8,128)}, f32[1024,512]{1,0:T(8,128)}) custom-call(f32[1024,512]{1,0:T(8,128)} %copy-done.2, f32[1024,512]{1,0:T(8,128)} %get-tuple-element.324.refs_1_, f32[4,8,16,128]{3,2,1,0:T(8,128)S(1)} %get-tuple-element.131.coef_ref.refs_2_), custom_call_target="tpu_custom_call" | custom-call | tf_op jit(solution)/shard_map/cond/branch_2_fun/pallas_call | solution.py:181
  248.6 3.1 copy.42
  253.3 7.2 %collective-permute-start.15 = (f32[1024,512]{1,0:T(8,128)}, f32[1024,512]{1,0:T(8,128)}, u32[]{:S(2)}, u32[]{:S(2)}) collective-permute-start(f32[1024,512]{1,0:T(8,128)} %get-tuple-element.153), channel_id=1, source_target_pairs={{0,16},{1,17},{2,18},{3,19},{4,20},{5,21},{6,22},{7,23},{8,24},{9,... | collective-permute-start | bytes 6291464 | tf_op jit(solution)/shard_map/ppermute | solution.py:20
  260.5 69.3 %conditional.8 = (f32[1024,512]{1,0:T(8,128)}) conditional(s32[]{:T(128)} %convert_element_type.23, f32[1024,512]{1,0:T(8,128)} %get-tuple-element.148, (f32[64,768]{1,0:T(8,128)S(1)}, f32[64,512]{1,0:T(8,128)S(1)}, f32[1024,512]{1,0:T(8,128)}) %tuple.233), branch_computations={%region_18.19_spmd, %region_19.21_spmd} | conditional | flops 1611825152 | bytes 20447492 | solution.py:399
  260.6 15.2 %all_to_all.23 = f32[4,64,768]{2,1,0:T(8,128)S(1)} all-to-all(f32[4,64,768]{2,1,0:T(8,128)S(1)} %broadcast_in_dim.164), channel_id=1, replica_groups={{0,2,4,6},{1,3,5,7},{8,10,12,14},{9,11,13,15},{16,18,20,22},{17,19,21,2..., dimensions={0} | all-to-all | bytes 1572864 | tf_op jit(solution)/shard_map/cond/branch_1_fun/all_to_all | solution.py:31
  275.8 4.6 %collective-permute-start.11 = (f32[256,512]{1,0:T(8,128)S(1)}, f32[256,512]{1,0:T(8,128)}, u32[]{:S(2)}, u32[]{:S(2)}) collective-permute-start(f32[256,512]{1,0:T(8,128)S(1)} %bitcast.243), channel_id=1, source_target_pairs={{0,1},{1,0},{2,3},{3,2},{4,5},{5,4},{6,7},{7,6},{8,9},{9,8},{10,11... | collective-permute-start | bytes 1572872 | tf_op jit(solution)/shard_map/cond/branch_1_fun/ppermute | solution.py:20
  284.6 3.9 all-to-all-start.1
  289.8 9.1 %all-to-all-done.1 = f32[4,64,768]{2,1,0:T(8,128)S(1)} async-done(((f32[4,64,768]{2,1,0:T(8,128)}), f32[4,64,768]{2,1,0:T(8,128)S(1)}, u32[]{:S(2)}, u32[]{:S(2)}) %all-to-all-start.1) | async-done | bytes 786464 | tf_op jit(solution)/shard_map/cond/branch_1_fun/all_to_all | solution.py:31
  299.0 26.0 %branch_1_fun.5 = f32[256,512]{1,0:T(8,128)S(1)} custom-call(f32[256,256]{1,0:T(8,128)S(1)} %slice.660.square, f32[256,512]{1,0:T(8,128)S(1)} %slice.661.given), custom_call_target="tpu_custom_call" | custom-call | tf_op jit(solution)/shard_map/cond/branch_1_fun/pallas_call | solution.py:265
  325.0 4.8 %convolution_subtract_fusion = f32[1024,512]{1,0:T(8,128)} fusion(f32[1024,512]{1,0:T(8,128)} %get-tuple-element.137, f32[256,512]{1,0:T(8,128)S(1)} %branch_1_fun.5, f32[256,512]{1,0:T(8,128)S(1)} %get-tuple-element.251, f32[256,512]{1,0:T(8,128)S(1)} %get-tuple-element.250), kind=kOutput, calls=%fused_computation.113 | convolution fusion | flops 1611399168 | bytes 5767168 | tf_op jit(solution)/shard_map/cond/branch_1_fun/dot_general | solution.py:396
  329.7 117.1 %collective-permute-done.15 = f32[1024,512]{1,0:T(8,128)} collective-permute-done((f32[1024,512]{1,0:T(8,128)}, f32[1024,512]{1,0:T(8,128)}, u32[]{:S(2)}, u32[]{:S(2)}) %collective-permute-start.15) | collective-permute-done | bytes 2097184 | tf_op jit(solution)/shard_map/ppermute | solution.py:20
  446.9 4.0 add.462
  (59 shorter events, 23.2 us)
Async XLA Ops:
  7.1 12.2 %copy-start = (f32[1024,512]{1,0:T(8,128)S(1)}, f32[1024,512]{1,0:T(8,128)}, u32[]{:S(2)}) copy-start(f32[1024,512]{1,0:T(8,128)} %param.21) | copy-start | bytes 6291460
  12.4 19.5 %all-to-all-start.2 = ((f32[16,16,512]{2,1,0:T(8,128)}), f32[16,16,512]{2,1,0:T(8,128)S(1)}, u32[]{:S(2)}, u32[]{:S(2)}) async-start(f32[16,16,512]{2,1,0:T(8,128)} %bitcast.110), calls=%async_computation.2 | async-start | bytes 1048576 | tf_op jit(solution)/shard_map/all_to_all | solution.py:358
  19.4 54.7 %collective-permute-start.13 = (f32[1024,512]{1,0:T(8,128)S(1)}, f32[1024,512]{1,0:T(8,128)}, u32[]{:S(2)}, u32[]{:S(2)}) collective-permute-start(f32[1024,512]{1,0:T(8,128)S(1)} %copy-done), channel_id=1, source_target_pairs={{0,256},{32,288},{64,320},{96,352},{128,384},{160,416},{192,448},{... | collective-permute-start | bytes 6291464 | tf_op jit(solution)/shard_map/ppermute | solution.py:20
  33.6 24.8 %all-to-all-start.3 = ((f32[4,16,768]{2,1,0:T(8,128)}), f32[4,16,768]{2,1,0:T(8,128)S(1)}, u32[]{:S(2)}, u32[]{:S(2)}) async-start(f32[4,16,768]{2,1,0:T(8,128)} %broadcast_in_dim.242), calls=%async_computation.3 | async-start | bytes 393216 | tf_op jit(solution)/shard_map/all_to_all | solution.py:31
  58.5 6.9 %collective-permute-start.1 = (f32[32,512]{1,0:T(8,128)S(1)}, f32[32,512]{1,0:T(8,128)}, u32[]{:S(2)}, u32[]{:S(2)}) collective-permute-start(f32[32,512]{1,0:T(8,128)S(1)} %param.3), channel_id=1, source_target_pairs={{0,4},{1,5},{2,6},{3,7},{4,0},{5,1},{6,2},{7,3},{8,12},{9,13},{10,... | collective-permute-start | bytes 196616 | tf_op jit(solution)/shard_map/cond/branch_2_fun/cond/branch_1_fun/ppermute | solution.py:20
  69.2 8.4 %all-to-all-start.4 = ((f32[4,16,768]{2,1,0:T(8,128)}), f32[4,16,768]{2,1,0:T(8,128)S(1)}, u32[]{:S(2)}, u32[]{:S(2)}) async-start(f32[4,16,768]{2,1,0:T(8,128)} %broadcast_in_dim.243), calls=%async_computation.4 | async-start | bytes 393216 | tf_op jit(solution)/shard_map/all_to_all | solution.py:31
  77.7 175.6 %collective-permute-start.14 = (f32[64,512]{1,0:T(8,128)S(1)}, f32[64,512]{1,0:T(8,128)S(1)}, u32[]{:S(2)}, u32[]{:S(2)}) collective-permute-start(f32[64,512]{1,0:T(8,128)S(1)} %slice.680), channel_id=1, source_target_pairs={{0,0},{1,1},{2,32},{3,33},{4,64},{5,65},{6,96},{7,97},{8,128},{9,1... | collective-permute-start | bytes 393224 | tf_op jit(solution)/shard_map/ppermute | solution.py:301
  86.7 1.3 copy-start.1
  95.2 94.3 %collective-permute-start.5 = (f32[1024,512]{1,0:T(8,128)S(1)}, f32[1024,512]{1,0:T(8,128)}, u32[]{:S(2)}, u32[]{:S(2)}) collective-permute-start(f32[1024,512]{1,0:T(8,128)S(1)} %param.9), channel_id=1, source_target_pairs={{0,64},{32,96},{64,0},{96,32},{128,192},{160,224},{192,128},{224,1... | collective-permute-start | bytes 6291464 | tf_op jit(solution)/shard_map/cond/branch_2_fun/cond/branch_1_fun/ppermute | solution.py:20
  191.6 1.3 copy-start.2
  192.9 49.0 %collective-permute-start.8 = (f32[1024,512]{1,0:T(8,128)S(1)}, f32[1024,512]{1,0:T(8,128)}, u32[]{:S(2)}, u32[]{:S(2)}) collective-permute-start(f32[1024,512]{1,0:T(8,128)S(1)} %param.12), channel_id=1, source_target_pairs={{0,4},{1,5},{2,6},{3,7},{4,0},{5,1},{6,2},{7,3},{8,12},{9,13},{10,... | collective-permute-start | bytes 6291464 | tf_op jit(solution)/shard_map/cond/branch_2_fun/cond/branch_1_fun/ppermute | solution.py:20
  253.3 193.6 %collective-permute-start.15 = (f32[1024,512]{1,0:T(8,128)}, f32[1024,512]{1,0:T(8,128)}, u32[]{:S(2)}, u32[]{:S(2)}) collective-permute-start(f32[1024,512]{1,0:T(8,128)} %get-tuple-element.153), channel_id=1, source_target_pairs={{0,16},{1,17},{2,18},{3,19},{4,20},{5,21},{6,22},{7,23},{8,24},{9,... | collective-permute-start | bytes 6291464 | tf_op jit(solution)/shard_map/ppermute | solution.py:20
  275.8 12.7 %collective-permute-start.11 = (f32[256,512]{1,0:T(8,128)S(1)}, f32[256,512]{1,0:T(8,128)}, u32[]{:S(2)}, u32[]{:S(2)}) collective-permute-start(f32[256,512]{1,0:T(8,128)S(1)} %bitcast.243), channel_id=1, source_target_pairs={{0,1},{1,0},{2,3},{3,2},{4,5},{5,4},{6,7},{7,6},{8,9},{9,8},{10,11... | collective-permute-start | bytes 1572872 | tf_op jit(solution)/shard_map/cond/branch_1_fun/ppermute | solution.py:20
  280.5 3.1 collective-permute-start.12
  284.6 14.2 %all-to-all-start.1 = ((f32[4,64,768]{2,1,0:T(8,128)}), f32[4,64,768]{2,1,0:T(8,128)S(1)}, u32[]{:S(2)}, u32[]{:S(2)}) async-start(f32[4,64,768]{2,1,0:T(8,128)} %broadcast_in_dim.165), calls=%async_computation.1 | async-start | bytes 1572864 | tf_op jit(solution)/shard_map/cond/branch_1_fun/all_to_all | solution.py:31

commit v3 on v2

--- a/solution.py
+++ b/solution.py
@@ -18,6 +18,12 @@
 def swap(value, axis, mask):
     pairs = [(source, source ^ mask) for source in range(lax.axis_size(axis))]
     return lax.ppermute(value, axis, pairs)
+
+
+def z_hi_groups():
+    size = lax.axis_size("col")
+    rest = size // Z_HI
+    return [list(range(low, size, rest)) for low in range(rest)]
 
 
 def gather(value, axis, stride, count):
@@ -102,7 +108,8 @@
         return values
 
     for n, values in enumerate(
-        (row_of(0), row_of(Plan.top_bit), col_of(), row_of(Plan.third_bit))
+        (row_of(0), row_of(Plan.top_bit), col_of(), row_of(Plan.third_bit),
+         row_of(Plan.top_bit | Plan.third_bit))
     ):
         for m in range(count):
             out[n, m] = values[m]
@@ -111,7 +118,7 @@
 def coefficients(top, col_blocks, info, angles):
     return pl.pallas_call(
         functools.partial(coefficients_kernel, Plan.count, top, col_blocks),
-        out_shape=jax.ShapeDtypeStruct((4, Plan.count, 16, 128), jnp.float32),
+        out_shape=jax.ShapeDtypeStruct((5, Plan.count, 16, 128), jnp.float32),
         in_specs=[SMEM, VMEM],
         out_specs=VMEM,
         compiler_params=pltpu.CompilerParams(vmem_limit_bytes=32 * 2**20),
@@ -186,6 +193,32 @@
         out_specs=[block] * 2,
         compiler_params=pltpu.CompilerParams(vmem_limit_bytes=48 * 2**20),
     )(*parts, coef)
+
+
+def deep_kernel(plan, place, field_ref, coef_ref, out_ref):
+    tables = (0, 3, 1, 4)
+    for to in range(4):
+        for j in range(plan.col_blocks):
+            total = None
+            for m in range(plan.count):
+                i = j ^ (m & 1)
+                term = field_ref[place[0] ^ (m >> 1), :, 128 * i : 128 * i + 128]
+                term = term * coef_ref[tables[to], m, 8 + j : 9 + j, :]
+                total = term if total is None else total + term
+            out_ref[place[0] ^ to, :, 128 * j : 128 * j + 128] = total
+
+
+def mix_deep(plan, place, field, coef, strip=64):
+    count, height, width = field.shape
+    block = pl.BlockSpec((count, strip, width), lambda i: (0, i, 0))
+    return pl.pallas_call(
+        functools.partial(deep_kernel, plan),
+        grid=(height // strip,),
+        out_shape=jax.ShapeDtypeStruct(field.shape, jnp.float32),
+        in_specs=[SMEM, block, VMEM],
+        out_specs=block,
+        compiler_params=pltpu.CompilerParams(vmem_limit_bytes=48 * 2**20),
+    )(place, field, coef)
 
 
 def near_kernel(plan, near_ref, top_ref, coef_ref, mine, theirs, middle):
@@ -342,11 +375,14 @@
     thirds = [1 << n for n in range(1, top.bit_length() - 1)]
     near = [t for t in thirds if t < min(row_blocks, col_blocks)]
     side = [t for t in thirds if col_blocks <= t < row_blocks]
-    away = [t for t in thirds if t >= max(row_blocks, col_blocks)]
-    plans = [Plan(group, top, row_blocks, col_blocks) for group in (near, side, away)]
+    cores = lax.axis_size("col") // (Z_HI * Y)
+    inner_z = col_blocks * cores * Y
+    away = [t for t in thirds if max(row_blocks, col_blocks) <= t < inner_z]
+    deep = [t for t in thirds if t >= inner_z]
+    plans = [Plan(group, top, row_blocks, col_blocks) for group in (near, side, away, deep)]
     inner = (given > 1) & (given < top)
     third = jnp.where(inner, given, near[0])
-    index = (third >= side[0]).astype(jnp.int32) + (third >= away[0]).astype(jnp.int32)
+    index = sum((third >= group[0]).astype(jnp.int32) for group in (side, away, deep))
     rb = lax.axis_index("row").astype(jnp.int32) * row_blocks
     cb = lax.axis_index("col").astype(jnp.int32) * col_blocks
     info = jnp.concatenate([delays // QUANTUM, rb[None], cb[None], third[None]]).astype(jnp.int32)
@@ -359,7 +395,6 @@
     over = swap(covariance, "row", top // row_blocks)
     piece = jnp.sum(spread, axis=0)
     block = jnp.dot(piece, sel_c.T, precision=HIGHEST)
-    cores = lax.axis_size("col") // (Z_HI * Y)
     along = gather(jnp.concatenate([piece, block], axis=1), "col", cores * Y, Z_HI)
     z_hi = lax.axis_index("col") // (cores * Y)
     apart = top // col_blocks // (cores * Y)
@@ -371,15 +406,6 @@
     quarter = gather(jnp.concatenate([mixed, block], axis=1), "row", 1, Z_LO)
     over, quarter = lax.optimization_barrier((over, quarter))
     quarter = quarter.reshape(-1, cols_dev + 2 * PANEL)
-    flipped = transposed(quarter[:, :cols_dev])
-    mine, moving = lax.switch(
-        index,
-        [functools.partial(mix_field, plan) for plan in plans],
-        covariance, over, coef, third,
-    )
-    moving, quarter, flipped = lax.optimization_barrier((moving, quarter, flipped))
-
-    arrived = swap(moving, "col", top // col_blocks)
 
     def finish(quarter, flipped, mine):
         pieces = jnp.concatenate([quarter[:, cols_dev:], flipped], axis=1)
@@ -396,11 +422,39 @@
         update = lax.dot_general(columns, weights, (((0,), (0,)), ((), ())), precision=HIGHEST)
         return mine - update
 
-    rest = lax.cond(
-        panel[0] >= 0, finish, lambda quarter, flipped, mine: mine,
-        quarter, flipped, mine,
-    )
-    return rest + arrived
+    def close(quarter, flipped, mine):
+        return lax.cond(
+            panel[0] >= 0, finish, lambda quarter, flipped, mine: mine, quarter, flipped, mine
+        )
+
+    def plain(covariance, over, quarter, coef):
+        flipped = transposed(quarter[:, :cols_dev])
+        mine, moving = lax.switch(
+            index,
+            [functools.partial(mix_field, plan) for plan in plans[:3]],
+            covariance, over, coef, third,
+        )
+        arrived = swap(moving, "col", top // col_blocks)
+        return close(quarter, flipped, mine) + arrived
+
+    def through(covariance, over, quarter, coef):
+        plan = plans[3]
+        flipped = transposed(quarter[:, :cols_dev])
+        mine, theirs = mix_rows(plan, covariance, over, coef)
+        field = mine + swap(theirs, "row", plan.third // row_blocks)
+        field, flipped = lax.optimization_barrier((field, flipped))
+        field = field.reshape(Z_HI, -1, cols_dev)
+        field = lax.all_to_all(field, "col", 0, 0, axis_index_groups=z_hi_groups())
+        field = mix_deep(plan, z_hi.astype(jnp.int32)[None], field, coef)
+        field, quarter, flipped = lax.optimization_barrier((field, quarter, flipped))
+        parts = [lax.dynamic_index_in_dim(field, z_hi ^ k) for k in range(Z_HI)]
+        parts[1:] = [swap(parts[k], "col", k * cores * Y) for k in range(1, Z_HI)]
+        rest = close(quarter, flipped, jnp.zeros((rows_dev, cols_dev), jnp.float32))
+        for k, part in enumerate(parts):
+            field = lax.dynamic_update_slice(field, part, (z_hi ^ k, 0, 0))
+        return rest + field.reshape(rows_dev, cols_dev)
+
+    return lax.cond(index == 3, through, plain, covariance, over, quarter, coef)
 
 
 def solution(mesh):

time: 452 us -> 363 us (0.80)
  the two profiles are of different devices: /device:TPU:103 before, /device:TPU:352 now
where the time goes in v3:
time: 363 us; the launch traced here: 362 us
  waiting for transfers between devices  234 us (64%)
  starting transfers between devices  47.4 us (13%)
  Pallas kernels  32.8 us (9%)
  blocking collectives  17.6 us (5%)
  matrix products  11 us (3%)
  local copies, waits for them, and re-layouts  8.29 us (2%)
  other arithmetic  6.83 us (2%)
    ppermute x1, waiting for transfers between devices, transposed(): return lax.ppermute(value, ('row', 'col'), pairs)  193 us
    pallas_call x1, Pallas kernels, solve_weights(): pl.pallas_call(weights_kernel, out_shape=jax.ShapeDtypeStruct(given.shape...  26 us
    all_to_all x3, starting transfers between devices, gather(): return lax.all_to_all(many, axis, 0, 0, axis_index_groups=groups)  21.8 us
    all_to_all x3, waiting for transfers between devices, gather(): return lax.all_to_all(many, axis, 0, 0, axis_index_groups=groups)  19.1 us
    all_to_all x1, blocking collectives, gather(): return lax.all_to_all(many, axis, 0, 0, axis_index_groups=groups)  17.6 us
    ppermute x4, waiting for transfers between devices, swap(): return lax.ppermute(value, axis, pairs)  14.8 us
    ppermute x4, starting transfers between devices, swap(): return lax.ppermute(value, axis, pairs)  11.4 us
    all_to_all x1, starting transfers between devices, shards(): spread = lax.all_to_all(part.reshape(n_row, -1, cols_dev), 'row', 0, 0)  7.57 us
  transfers between devices with their start and end apart: 9, of which 6 were waited for; matrix products, arithmetic and copies ran while one was open for 3% of the time, Pallas kernels for 7%

profile of v3, /device:TPU:352, one launch (start us, length us, event | category | flops | bytes accessed | tf_op | source)
XLA Modules:
  0.0 362.3 jit_solution(18261479041525093196)
XLA Ops:
  0.0 1.3 and_select_fusion
  3.9 1.0 reshape.244.angles
  5.0 1.4 shard_map.48
  7.2 5.3 %fusion.8 = f32[256,512]{1,0:T(8,128)} fusion(f32[1024,512]{1,0:T(8,128)} %param.23, f32[1024]{0:T(1024)S(1)} %get-tuple-element.354, s32[1024]{0:T(1024)S(1)} %get-tuple-element.364, f32[1024]{0:T(1024)S(1)} %get-tuple-element.355, s32[1024]{0:T(1024)S(1)} %get-tuple-element.365, f32[1024]{0:T(1024)S(1)} %get-tuple-element.356, ...), kind=kOutput, calls=%fused_computation.179 | convolution fusion | flops 1616642048 | bytes 2688000 | tf_op jit(solution)/shard_map/dot_general | solution.py:393
  12.4 7.6 %all-to-all-start.5 = ((f32[16,16,512]{2,1,0:T(8,128)}), f32[16,16,512]{2,1,0:T(8,128)S(1)}, u32[]{:S(2)}, u32[]{:S(2)}) async-start(f32[16,16,512]{2,1,0:T(8,128)} %bitcast.149), calls=%async_computation.5 | async-start | bytes 1048576 | tf_op jit(solution)/shard_map/all_to_all | solution.py:394
  20.0 4.9 %collective-permute-start.20 = (f32[1024,512]{1,0:T(8,128)S(1)}, f32[1024,512]{1,0:T(8,128)}, u32[]{:S(2)}, u32[]{:S(2)}) collective-permute-start(f32[1024,512]{1,0:T(8,128)S(1)} %copy-done.2), channel_id=1, source_target_pairs={{0,256},{32,288},{64,320},{96,352},{128,384},{160,416},{192,448},{... | collective-permute-start | bytes 6291464 | tf_op jit(solution)/shard_map/ppermute | solution.py:20
  25.0 6.9 %all-to-all-done.5 = f32[16,16,512]{2,1,0:T(8,128)S(1)} async-done(((f32[16,16,512]{2,1,0:T(8,128)}), f32[16,16,512]{2,1,0:T(8,128)S(1)}, u32[]{:S(2)}, u32[]{:S(2)}) %all-to-all-start.5) | async-done | bytes 524320 | tf_op jit(solution)/shard_map/all_to_all | solution.py:394
  31.9 0.9 fusion.32
  33.5 12.0 %all-to-all-start.6 = ((f32[4,16,768]{2,1,0:T(8,128)}), f32[4,16,768]{2,1,0:T(8,128)S(1)}, u32[]{:S(2)}, u32[]{:S(2)}) async-start(f32[4,16,768]{2,1,0:T(8,128)} %broadcast_in_dim.257), calls=%async_computation.6 | async-start | bytes 393216 | tf_op jit(solution)/shard_map/all_to_all | solution.py:37
  45.5 7.2 %all-to-all-done.6 = f32[4,16,768]{2,1,0:T(8,128)S(1)} async-done(((f32[4,16,768]{2,1,0:T(8,128)}), f32[4,16,768]{2,1,0:T(8,128)S(1)}, u32[]{:S(2)}, u32[]{:S(2)}) %all-to-all-start.6) | async-done | bytes 196640 | tf_op jit(solution)/shard_map/all_to_all | solution.py:37
  53.7 6.3 %all-to-all-start.7 = ((f32[4,16,768]{2,1,0:T(8,128)}), f32[4,16,768]{2,1,0:T(8,128)S(1)}, u32[]{:S(2)}, u32[]{:S(2)}) async-start(f32[4,16,768]{2,1,0:T(8,128)} %broadcast_in_dim.258), calls=%async_computation.7 | async-start | bytes 393216 | tf_op jit(solution)/shard_map/all_to_all | solution.py:37
  60.0 14.0 %collective-permute-done.20 = f32[1024,512]{1,0:T(8,128)} collective-permute-done((f32[1024,512]{1,0:T(8,128)S(1)}, f32[1024,512]{1,0:T(8,128)}, u32[]{:S(2)}, u32[]{:S(2)}) %collective-permute-start.20) | collective-permute-done | bytes 2097184 | tf_op jit(solution)/shard_map/ppermute | solution.py:20
  74.0 288.3 %conditional.9 = (f32[1024,512]{1,0:T(8,128)}) conditional(s32[]{:T(128)} %convert_element_type.34, (s32[1]{0:T(128)}, s32[]{:T(128)}, f32[1024,512]{1,0:T(8,128)S(1)}, f32[1024,512]{1,0:T(8,128)}, f32[5,8,16,128]{3,2,1,0:T(8,128)S(1)}, /*index=5*/s32[]{:T(128)}, f32[64,768]{1,0:T(8,128)S(1)}) %tuple.271, (s32[1]{0:T(128)}, s32[]{:T(128)}, ...), branch_computations={%region_9.20_spmd, %region_20.24_spmd} | conditional | flops 1612873728 | bytes 89391992 | solution.py:457
  74.0 10.1 %conditional.3 = (f32[1024,512]{1,0:T(8,128)}, f32[1024,512]{1,0:T(8,128)}, f32[1024,512]{1,0:T(8,128)S(1)}, f32[1024,512]{1,0:T(8,128)}) conditional(s32[]{:T(128)} %clamp.11, (f32[1024,512]{1,0:T(8,128)S(1)}, f32[1024,512]{1,0:T(8,128)}, f32[5,8,16,128]{3,2,1,0:T(8,128)S(1)}) %tuple.74, (f32[1024,512]{1,0:T(8,128)S(1)}, ...), branch_computations={%region_10.10_spmd, %region_11.11_spmd, %region_12.16_spmd} | conditional | flops 524291 | bytes 48234712 | solution.py:432
  74.0 5.3 %branch_0_fun.1 = (f32[1024,512]{1,0:T(8,128)}, f32[1024,512]{1,0:T(8,128)}) custom-call(f32[1024,512]{1,0:T(8,128)S(1)} %get-tuple-element.159.near_ref, f32[1024,512]{1,0:T(8,128)} %get-tuple-element.160.top_ref, f32[5,8,16,128]{3,2,1,0:T(8,128)S(1)} %get-tuple-element.161.coef_ref), custom_call_target="tpu_custom_call" | custom-call | tf_op jit(solution)/shard_map/cond/branch_0_fun/cond/branch_0_fun/pallas_call | solution.py:235
  79.3 3.1 copy.46
  82.5 1.6 copy.47
  84.0 2.2 collective-permute-start.12
  86.3 6.6 %collective-permute-start.11 = (f32[64,512]{1,0:T(8,128)S(1)}, f32[64,512]{1,0:T(8,128)S(1)}, u32[]{:S(2)}, u32[]{:S(2)}) collective-permute-start(f32[64,512]{1,0:T(8,128)S(1)} %slice.772), channel_id=1, source_target_pairs={{0,0},{1,1},{2,32},{3,33},{4,64},{5,65},{6,96},{7,97},{8,128},{9,1... | collective-permute-start | bytes 393224 | tf_op jit(solution)/shard_map/cond/branch_0_fun/ppermute | solution.py:334
  93.5 193.2 %collective-permute-done.11 = f32[64,512]{1,0:T(8,128)S(1)} collective-permute-done((f32[64,512]{1,0:T(8,128)S(1)}, f32[64,512]{1,0:T(8,128)S(1)}, u32[]{:S(2)}, u32[]{:S(2)}) %collective-permute-start.11) | collective-permute-done | bytes 131104 | tf_op jit(solution)/shard_map/cond/branch_0_fun/ppermute | solution.py:334
  286.8 71.4 %conditional.4 = (f32[1024,512]{1,0:T(8,128)}) conditional(s32[]{:T(128)} %bitcast.130, f32[1024,512]{1,0:T(8,128)} %get-tuple-element.186, (f32[64,768]{1,0:T(8,128)S(1)}, f32[64,512]{1,0:T(8,128)S(1)}, f32[1024,512]{1,0:T(8,128)}) %tuple.77), branch_computations={%region_17.17_spmd, %region_18.19_spmd} | conditional | flops 1611825152 | bytes 20447492 | solution.py:426
  286.9 17.6 %all_to_all.35 = f32[4,64,768]{2,1,0:T(8,128)S(1)} all-to-all(f32[4,64,768]{2,1,0:T(8,128)S(1)} %broadcast_in_dim.176), channel_id=1, replica_groups={{0,2,4,6},{1,3,5,7},{8,10,12,14},{9,11,13,15},{16,18,20,22},{17,19,21,2..., dimensions={0} | all-to-all | bytes 1572864 | tf_op jit(solution)/shard_map/cond/branch_0_fun/cond/branch_1_fun/all_to_all | solution.py:37
  304.5 1.9 collective-permute-start.9
  306.5 2.4 collective-permute-start.10
  308.9 0.9 collective-permute-done.10
  309.8 0.9 broadcast_in_dim.177
  310.8 3.5 all-to-all-start.1
  314.3 1.2 broadcast_select_fusion.1
  315.5 11.8 %all-to-all-done.1 = f32[4,64,768]{2,1,0:T(8,128)S(1)} async-done(((f32[4,64,768]{2,1,0:T(8,128)}), f32[4,64,768]{2,1,0:T(8,128)S(1)}, u32[]{:S(2)}, u32[]{:S(2)}) %all-to-all-start.1) | async-done | bytes 786464 | tf_op jit(solution)/shard_map/cond/branch_0_fun/cond/branch_1_fun/all_to_all | solution.py:37
  327.4 26.0 %branch_1_fun.8 = f32[256,512]{1,0:T(8,128)S(1)} custom-call(f32[256,256]{1,0:T(8,128)S(1)} %slice.842.square, f32[256,512]{1,0:T(8,128)S(1)} %slice.843.given), custom_call_target="tpu_custom_call" | custom-call | tf_op jit(solution)/shard_map/cond/branch_0_fun/cond/branch_1_fun/pallas_call | solution.py:298
  353.4 4.8 %convolution_subtract_fusion = f32[1024,512]{1,0:T(8,128)} fusion(f32[1024,512]{1,0:T(8,128)} %get-tuple-element.177, f32[256,512]{1,0:T(8,128)S(1)} %branch_1_fun.8, f32[256,512]{1,0:T(8,128)S(1)} %get-tuple-element.338, f32[256,512]{1,0:T(8,128)S(1)} %get-tuple-element.337), kind=kOutput, calls=%fused_computation.151 | convolution fusion | flops 1611399168 | bytes 5767168 | tf_op jit(solution)/shard_map/cond/branch_0_fun/cond/branch_1_fun/dot_general | solution.py:422
  358.2 4.0 %add.508 = f32[1024,512]{1,0:T(8,128)} add(f32[1024,512]{1,0:T(8,128)} %get-tuple-element.420, f32[1024,512]{1,0:T(8,128)} %collective-permute-done.12) | non-fusion elementwise | flops 524288 | bytes 6291456 | tf_op jit(solution)/shard_map/cond/branch_0_fun/add | solution.py:438
  (44 shorter events, 2.2 us)
Async XLA Ops:
  7.2 12.8 %copy-start.2 = (f32[1024,512]{1,0:T(8,128)S(1)}, f32[1024,512]{1,0:T(8,128)}, u32[]{:S(2)}) copy-start(f32[1024,512]{1,0:T(8,128)} %param.23) | copy-start | bytes 6291460
  12.4 19.4 %all-to-all-start.5 = ((f32[16,16,512]{2,1,0:T(8,128)}), f32[16,16,512]{2,1,0:T(8,128)S(1)}, u32[]{:S(2)}, u32[]{:S(2)}) async-start(f32[16,16,512]{2,1,0:T(8,128)} %bitcast.149), calls=%async_computation.5 | async-start | bytes 1048576 | tf_op jit(solution)/shard_map/all_to_all | solution.py:394
  20.0 54.0 %collective-permute-start.20 = (f32[1024,512]{1,0:T(8,128)S(1)}, f32[1024,512]{1,0:T(8,128)}, u32[]{:S(2)}, u32[]{:S(2)}) collective-permute-start(f32[1024,512]{1,0:T(8,128)S(1)} %copy-done.2), channel_id=1, source_target_pairs={{0,256},{32,288},{64,320},{96,352},{128,384},{160,416},{192,448},{... | collective-permute-start | bytes 6291464 | tf_op jit(solution)/shard_map/ppermute | solution.py:20
  33.5 19.2 %all-to-all-start.6 = ((f32[4,16,768]{2,1,0:T(8,128)}), f32[4,16,768]{2,1,0:T(8,128)S(1)}, u32[]{:S(2)}, u32[]{:S(2)}) async-start(f32[4,16,768]{2,1,0:T(8,128)} %broadcast_in_dim.257), calls=%async_computation.6 | async-start | bytes 393216 | tf_op jit(solution)/shard_map/all_to_all | solution.py:37
  53.7 20.3 %all-to-all-start.7 = ((f32[4,16,768]{2,1,0:T(8,128)}), f32[4,16,768]{2,1,0:T(8,128)S(1)}, u32[]{:S(2)}, u32[]{:S(2)}) async-start(f32[4,16,768]{2,1,0:T(8,128)} %broadcast_in_dim.258), calls=%async_computation.7 | async-start | bytes 393216 | tf_op jit(solution)/shard_map/all_to_all | solution.py:37
  84.0 274.2 %collective-permute-start.12 = (f32[1024,512]{1,0:T(8,128)}, f32[1024,512]{1,0:T(8,128)}, u32[]{:S(2)}, u32[]{:S(2)}) collective-permute-start(f32[1024,512]{1,0:T(8,128)} %get-tuple-element.188), channel_id=1, source_target_pairs={{0,16},{1,17},{2,18},{3,19},{4,20},{5,21},{6,22},{7,23},{8,24},{9,... | collective-permute-start | bytes 6291464 | tf_op jit(solution)/shard_map/cond/branch_0_fun/ppermute | solution.py:20
  86.3 200.5 %collective-permute-start.11 = (f32[64,512]{1,0:T(8,128)S(1)}, f32[64,512]{1,0:T(8,128)S(1)}, u32[]{:S(2)}, u32[]{:S(2)}) collective-permute-start(f32[64,512]{1,0:T(8,128)S(1)} %slice.772), channel_id=1, source_target_pairs={{0,0},{1,1},{2,32},{3,33},{4,64},{5,65},{6,96},{7,97},{8,128},{9,1... | collective-permute-start | bytes 393224 | tf_op jit(solution)/shard_map/cond/branch_0_fun/ppermute | solution.py:334
  304.5 9.7 %collective-permute-start.9 = (f32[256,512]{1,0:T(8,128)S(1)}, f32[256,512]{1,0:T(8,128)}, u32[]{:S(2)}, u32[]{:S(2)}) collective-permute-start(f32[256,512]{1,0:T(8,128)S(1)} %bitcast.322), channel_id=1, source_target_pairs={{0,1},{1,0},{2,3},{3,2},{4,5},{5,4},{6,7},{7,6},{8,9},{9,8},{10,11... | collective-permute-start | bytes 1572872 | tf_op jit(solution)/shard_map/cond/branch_0_fun/cond/branch_1_fun/ppermute | solution.py:20
  306.5 3.3 collective-permute-start.10
  310.8 16.6 %all-to-all-start.1 = ((f32[4,64,768]{2,1,0:T(8,128)}), f32[4,64,768]{2,1,0:T(8,128)S(1)}, u32[]{:S(2)}, u32[]{:S(2)}) async-start(f32[4,64,768]{2,1,0:T(8,128)} %broadcast_in_dim.177), calls=%async_computation.1 | async-start | bytes 1572864 | tf_op jit(solution)/shard_map/cond/branch_0_fun/cond/branch_1_fun/all_to_all | solution.py:37

commit v4 on v3

--- a/solution.py
+++ b/solution.py
@@ -404,10 +404,11 @@
         index, [functools.partial(mix_piece, plan) for plan in plans], piece, top_piece, coef, third
     )
     quarter = gather(jnp.concatenate([mixed, block], axis=1), "row", 1, Z_LO)
-    over, quarter = lax.optimization_barrier((over, quarter))
     quarter = quarter.reshape(-1, cols_dev + 2 * PANEL)
-
-    def finish(quarter, flipped, mine):
+    flipped = transposed(quarter[:, :cols_dev])
+    over, quarter, flipped = lax.optimization_barrier((over, quarter, flipped))
+
+    def finish(quarter, flipped):
         pieces = jnp.concatenate([quarter[:, cols_dev:], flipped], axis=1)
         pieces = gather(pieces, "col", cores, Y)
         block = jnp.sum(pieces[:, :, : 2 * PANEL], axis=0)
@@ -419,42 +420,38 @@
         weights = solve_weights(both[:, cols_dev:], both[:, :cols_dev])
         low = lax.axis_index("col") % 2 == 0
         columns = jnp.concatenate([jnp.where(low, here, twin), jnp.where(low, twin, here)], axis=1)
-        update = lax.dot_general(columns, weights, (((0,), (0,)), ((), ())), precision=HIGHEST)
-        return mine - update
-
-    def close(quarter, flipped, mine):
-        return lax.cond(
-            panel[0] >= 0, finish, lambda quarter, flipped, mine: mine, quarter, flipped, mine
-        )
-
-    def plain(covariance, over, quarter, coef):
-        flipped = transposed(quarter[:, :cols_dev])
+        return lax.dot_general(columns, weights, (((0,), (0,)), ((), ())), precision=HIGHEST)
+
+    def close(quarter, flipped):
+        def skip(quarter, flipped):
+            return jnp.zeros((rows_dev, cols_dev), jnp.float32)
+
+        return lax.cond(panel[0] >= 0, finish, skip, quarter, flipped)
+
+    def plain(covariance, over, quarter, flipped, coef):
         mine, moving = lax.switch(
             index,
             [functools.partial(mix_field, plan) for plan in plans[:3]],
             covariance, over, coef, third,
         )
         arrived = swap(moving, "col", top // col_blocks)
-        return close(quarter, flipped, mine) + arrived
-
-    def through(covariance, over, quarter, coef):
+        return mine + arrived - close(quarter, flipped)
+
+    def through(covariance, over, quarter, flipped, coef):
         plan = plans[3]
-        flipped = transposed(quarter[:, :cols_dev])
         mine, theirs = mix_rows(plan, covariance, over, coef)
         field = mine + swap(theirs, "row", plan.third // row_blocks)
-        field, flipped = lax.optimization_barrier((field, flipped))
         field = field.reshape(Z_HI, -1, cols_dev)
         field = lax.all_to_all(field, "col", 0, 0, axis_index_groups=z_hi_groups())
         field = mix_deep(plan, z_hi.astype(jnp.int32)[None], field, coef)
-        field, quarter, flipped = lax.optimization_barrier((field, quarter, flipped))
         parts = [lax.dynamic_index_in_dim(field, z_hi ^ k) for k in range(Z_HI)]
         parts[1:] = [swap(parts[k], "col", k * cores * Y) for k in range(1, Z_HI)]
-        rest = close(quarter, flipped, jnp.zeros((rows_dev, cols_dev), jnp.float32))
+        update = close(quarter, flipped)
         for k, part in enumerate(parts):
             field = lax.dynamic_update_slice(field, part, (z_hi ^ k, 0, 0))
-        return rest + field.reshape(rows_dev, cols_dev)
-
-    return lax.cond(index == 3, through, plain, covariance, over, quarter, coef)
+        return field.reshape(rows_dev, cols_dev) - update
+
+    return lax.cond(index == 3, through, plain, covariance, over, quarter, flipped, coef)
 
 
 def solution(mesh):

time: 363 us -> 314 us (0.87)
  the two profiles are of different devices: /device:TPU:352 before, /device:TPU:103 now
where the time goes in v4:
time: 314 us
  waiting for transfers between devices  177 us (56%)
  starting transfers between devices  51.8 us (16%)
  Pallas kernels  38.1 us (12%)
  blocking collectives  24.4 us (8%)
  matrix products  8 us (3%)
  other arithmetic  4.74 us (2%)
  local copies, waits for them, and re-layouts  4.19 us (1%)
  between operations  3.49 us (1%)
    ppermute x6, waiting for transfers between devices, swap(): return lax.ppermute(value, axis, pairs)  129 us
    pallas_call x1, Pallas kernels, solve_weights(): pl.pallas_call(weights_kernel, out_shape=jax.ShapeDtypeStruct(given.shape...  26 us
    all_to_all x2, blocking collectives, gather(): return lax.all_to_all(many, axis, 0, 0, axis_index_groups=groups)  24.4 us
    all_to_all x2, waiting for transfers between devices, gather(): return lax.all_to_all(many, axis, 0, 0, axis_index_groups=groups)  23.1 us
    ppermute x6, starting transfers between devices, swap(): return lax.ppermute(value, axis, pairs)  19.6 us
    all_to_all x2, starting transfers between devices, gather(): return lax.all_to_all(many, axis, 0, 0, axis_index_groups=groups)  18.7 us
    ppermute x1, waiting for transfers between devices, transposed(): return lax.ppermute(value, ('row', 'col'), pairs)  16.2 us
    all_to_all x1, waiting for transfers between devices, shards(): spread = lax.all_to_all(part.reshape(n_row, -1, cols_dev), 'row', 0, 0)  9.39 us
  transfers between devices with their start and end apart: 10, of which 8 were waited for; matrix products, arithmetic and copies ran while one was open for 2% of the time, Pallas kernels for 8%

profile of v4, /device:TPU:103, one launch (start us, length us, event | category | flops | bytes accessed | tf_op | source)
XLA Modules:
  0.0 313.8 jit_solution(2704239304228085275)
XLA Ops:
  0.0 1.3 and_select_fusion
  5.0 1.4 shard_map.48
  7.2 5.3 %fusion.10 = f32[256,512]{1,0:T(8,128)} fusion(f32[1024,512]{1,0:T(8,128)} %param.23, f32[1024]{0:T(1024)S(1)} %get-tuple-element.336, s32[1024]{0:T(1024)S(1)} %get-tuple-element.346, f32[1024]{0:T(1024)S(1)} %get-tuple-element.337, s32[1024]{0:T(1024)S(1)} %get-tuple-element.347, f32[1024]{0:T(1024)S(1)} %get-tuple-element.338, ...), kind=kOutput, calls=%fused_computation.180 | convolution fusion | flops 1616642048 | bytes 2688000 | tf_op jit(solution)/shard_map/dot_general | solution.py:393
  12.4 6.9 %all-to-all-start.5 = ((f32[16,16,512]{2,1,0:T(8,128)}), f32[16,16,512]{2,1,0:T(8,128)S(1)}, u32[]{:S(2)}, u32[]{:S(2)}) async-start(f32[16,16,512]{2,1,0:T(8,128)} %bitcast.149), calls=%async_computation.5 | async-start | bytes 1048576 | tf_op jit(solution)/shard_map/all_to_all | solution.py:394
  19.4 3.1 collective-permute-start.18
  22.6 9.4 %all-to-all-done.5 = f32[16,16,512]{2,1,0:T(8,128)S(1)} async-done(((f32[16,16,512]{2,1,0:T(8,128)}), f32[16,16,512]{2,1,0:T(8,128)S(1)}, u32[]{:S(2)}, u32[]{:S(2)}) %all-to-all-start.5) | async-done | bytes 524320 | tf_op jit(solution)/shard_map/all_to_all | solution.py:394
  33.6 12.2 %all-to-all-start.6 = ((f32[4,16,768]{2,1,0:T(8,128)}), f32[4,16,768]{2,1,0:T(8,128)S(1)}, u32[]{:S(2)}, u32[]{:S(2)}) async-start(f32[4,16,768]{2,1,0:T(8,128)} %broadcast_in_dim.257), calls=%async_computation.6 | async-start | bytes 393216 | tf_op jit(solution)/shard_map/all_to_all | solution.py:37
  45.8 12.6 %all-to-all-done.6 = f32[4,16,768]{2,1,0:T(8,128)S(1)} async-done(((f32[4,16,768]{2,1,0:T(8,128)}), f32[4,16,768]{2,1,0:T(8,128)S(1)}, u32[]{:S(2)}, u32[]{:S(2)}) %all-to-all-start.6) | async-done | bytes 196640 | tf_op jit(solution)/shard_map/all_to_all | solution.py:37
  58.4 7.7 %conditional.8 = (f32[16,512]{1,0:T(8,128)S(1)}) conditional(s32[]{:T(128)} %clamp.13, (f32[16,512]{1,0:T(8,128)S(1)}, f32[5,8,16,128]{3,2,1,0:T(8,128)S(1)}, f32[16,512]{1,0:T(8,128)S(1)}) %tuple.73, (f32[16,512]{1,0:T(8,128)S(1)}, f32[5,8,16,128]{3,2,1,0:T(8,128)S(1)}, f32[16,512]{1,0:T(8,128)S(1)}) %tuple.73, ...), branch_computations={%region_2.3_spmd, %region_3.4_spmd, %region_4.7_spmd, %region_7.8_... | conditional | flops 163843 | bytes 802902 | solution.py:403
  58.5 6.7 %collective-permute-start.7 = (f32[32,512]{1,0:T(8,128)S(1)}, f32[32,512]{1,0:T(8,128)S(1)}, u32[]{:S(2)}, u32[]{:S(2)}) collective-permute-start(f32[32,512]{1,0:T(8,128)S(1)} %pad_maximum_fusion.1), channel_id=1, source_target_pairs={{0,1},{1,0},{2,3},{3,2},{4,5},{5,4},{6,7},{7,6},{8,9},{9,8},{10,11... | collective-permute-start | bytes 196616 | tf_op jit(solution)/shard_map/cond/branch_1_fun/ppermute | solution.py:20
  66.2 9.9 %all_to_all.37 = f32[4,16,768]{2,1,0:T(8,128)S(1)} all-to-all(f32[4,16,768]{2,1,0:T(8,128)S(1)} %broadcast_in_dim.258), channel_id=1, replica_groups={{0,32,64,96},{128,160,192,224},{256,288,320,352},{384,416,448,480},{1,3..., dimensions={0} | all-to-all | bytes 393216 | tf_op jit(solution)/shard_map/all_to_all | solution.py:37
  76.1 6.5 %collective-permute-start.19 = (f32[64,512]{1,0:T(8,128)S(1)}, f32[64,512]{1,0:T(8,128)S(1)}, u32[]{:S(2)}, u32[]{:S(2)}) collective-permute-start(f32[64,512]{1,0:T(8,128)S(1)} %slice.864), channel_id=1, source_target_pairs={{0,0},{1,1},{2,32},{3,33},{4,64},{5,65},{6,96},{7,97},{8,128},{9,1... | collective-permute-start | bytes 393224 | tf_op jit(solution)/shard_map/ppermute | solution.py:334
  82.6 16.2 %collective-permute-done.19 = f32[64,512]{1,0:T(8,128)S(1)} collective-permute-done((f32[64,512]{1,0:T(8,128)S(1)}, f32[64,512]{1,0:T(8,128)S(1)}, u32[]{:S(2)}, u32[]{:S(2)}) %collective-permute-start.19) | collective-permute-done | bytes 131104 | tf_op jit(solution)/shard_map/ppermute | solution.py:334
  98.8 213.7 %conditional.9 = (f32[1024,512]{1,0:T(8,128)S(1)}) conditional(s32[]{:T(128)} %convert_element_type.34, (s32[]{:T(128)}, f32[1024,512]{1,0:T(8,128)S(1)}, f32[1024,512]{1,0:T(8,128)}, f32[5,8,16,128]{3,2,1,0:T(8,128)S(1)}, s32[]{:T(128)}, /*index=5*/s32[1]{0:T(128)}, f32[64,768]{1,0:T(8,128)S(1)}, f32[64,512]{1,0:T(8,128)S(1)}) %tuple.252, ...), branch_computations={%region_9.20_spmd, %region_20.24_spmd} | conditional | flops 1612873728 | bytes 88605512 | solution.py:454
  98.8 17.2 %conditional.3 = ((f32[1024,512]{1,0:T(8,128)}, f32[1024,512]{1,0:T(8,128)})) conditional(s32[]{:T(128)} %clamp.11, (f32[1024,512]{1,0:T(8,128)S(1)}, f32[1024,512]{1,0:T(8,128)}, f32[5,8,16,128]{3,2,1,0:T(8,128)S(1)}) %tuple.59, (f32[1024,512]{1,0:T(8,128)S(1)}, f32[1024,512]{1,0:T(8,128)}, ...), branch_computations={%region_10.10_spmd, %region_11.11_spmd, %region_12.16_spmd} | conditional | flops 524291 | bytes 39846080 | solution.py:432
  98.8 7.0 %branch_1_fun.6.refs_0_ = f32[1024,512]{1,0:T(8,128)S(1)} custom-call(f32[1024,512]{1,0:T(8,128)S(1)} %get-tuple-element.152.near_ref, f32[1024,512]{1,0:T(8,128)} %get-tuple-element.153.top_ref, f32[5,8,16,128]{3,2,1,0:T(8,128)S(1)} %get-tuple-element.154.coef_ref.refs_2_), custom_call_target="tpu_custom_call" | custom-call | tf_op jit(solution)/shard_map/cond/branch_0_fun/cond/branch_1_fun/pallas_call | solution.py:153
  105.8 2.8 collective-permute-start.2
  108.6 3.8 %collective-permute-done.2.refs_1_ = f32[1024,512]{1,0:T(8,128)S(1)} collective-permute-done((f32[1024,512]{1,0:T(8,128)S(1)}, f32[1024,512]{1,0:T(8,128)S(1)}, u32[]{:S(2)}, u32[]{:S(2)}) %collective-permute-start.2) | collective-permute-done | bytes 2097184 | tf_op jit(solution)/shard_map/cond/branch_0_fun/cond/branch_1_fun/ppermute | solution.py:20
  112.4 3.7 %branch_1_fun.7 = (f32[1024,512]{1,0:T(8,128)}, f32[1024,512]{1,0:T(8,128)}) custom-call(f32[1024,512]{1,0:T(8,128)S(1)} %branch_1_fun.6.refs_0_, f32[1024,512]{1,0:T(8,128)S(1)} %collective-permute-done.2.refs_1_, f32[5,8,16,128]{3,2,1,0:T(8,128)S(1)} %get-tuple-element.154.coef_ref.refs_2_), custom_call_target="tpu_custom_call" | custom-call | tf_op jit(solution)/shard_map/cond/branch_0_fun/cond/branch_1_fun/pallas_call | solution.py:188
  116.0 1.9 collective-permute-start.11
  118.6 67.4 %conditional.4 = (f32[1024,512]{1,0:T(8,128)S(1)}) conditional(s32[]{:T(128)} %bitcast.130, () %tuple.62, (f32[64,768]{1,0:T(8,128)S(1)}, f32[64,512]{1,0:T(8,128)S(1)}) %tuple.63), branch_computations={%region_17.17_spmd, %region_18.19_spmd} | conditional | flops 1611300864 | bytes 18350340 | solution.py:429
  118.7 14.6 %all_to_all.35 = f32[4,64,768]{2,1,0:T(8,128)S(1)} all-to-all(f32[4,64,768]{2,1,0:T(8,128)S(1)} %broadcast_in_dim.176), channel_id=1, replica_groups={{0,2,4,6},{1,3,5,7},{8,10,12,14},{9,11,13,15},{16,18,20,22},{17,19,21,2..., dimensions={0} | all-to-all | bytes 1572864 | tf_op jit(solution)/shard_map/cond/branch_0_fun/cond/branch_1_fun/all_to_all | solution.py:37
  133.3 3.2 %collective-permute-start.9 = (f32[256,512]{1,0:T(8,128)S(1)}, f32[256,512]{1,0:T(8,128)S(1)}, u32[]{:S(2)}, u32[]{:S(2)}) collective-permute-start(f32[256,512]{1,0:T(8,128)S(1)} %bitcast.323), channel_id=1, source_target_pairs={{0,1},{1,0},{2,3},{3,2},{4,5},{5,4},{6,7},{7,6},{8,9},{9,8},{10,11... | collective-permute-start | bytes 1572872 | tf_op jit(solution)/shard_map/cond/branch_0_fun/cond/branch_1_fun/ppermute | solution.py:20
  136.5 1.9 collective-permute-start.10
  138.5 1.2 collective-permute-done.10
  140.6 6.5 %all-to-all-start.1 = ((f32[4,64,768]{2,1,0:T(8,128)}), f32[4,64,768]{2,1,0:T(8,128)S(1)}, u32[]{:S(2)}, u32[]{:S(2)}) async-start(f32[4,64,768]{2,1,0:T(8,128)} %broadcast_in_dim.177), calls=%async_computation.1 | async-start | bytes 1572864 | tf_op jit(solution)/shard_map/cond/branch_0_fun/cond/branch_1_fun/all_to_all | solution.py:37
  147.3 10.5 %all-to-all-done.1 = f32[4,64,768]{2,1,0:T(8,128)S(1)} async-done(((f32[4,64,768]{2,1,0:T(8,128)}), f32[4,64,768]{2,1,0:T(8,128)S(1)}, u32[]{:S(2)}, u32[]{:S(2)}) %all-to-all-start.1) | async-done | bytes 786464 | tf_op jit(solution)/shard_map/cond/branch_0_fun/cond/branch_1_fun/all_to_all | solution.py:37
  157.9 26.0 %branch_1_fun.8 = f32[256,512]{1,0:T(8,128)S(1)} custom-call(f32[256,256]{1,0:T(8,128)S(1)} %slice.840.square, f32[256,512]{1,0:T(8,128)S(1)} %slice.841.given), custom_call_target="tpu_custom_call" | custom-call | tf_op jit(solution)/shard_map/cond/branch_0_fun/cond/branch_1_fun/pallas_call | solution.py:298
  183.9 1.8 fusion
  185.9 122.9 %collective-permute-done.11 = f32[1024,512]{1,0:T(8,128)} collective-permute-done((f32[1024,512]{1,0:T(8,128)}, f32[1024,512]{1,0:T(8,128)}, u32[]{:S(2)}, u32[]{:S(2)}) %collective-permute-start.11) | collective-permute-done | bytes 2097184 | tf_op jit(solution)/shard_map/cond/branch_0_fun/ppermute | solution.py:20
  308.9 3.0 add_subtract_fusion
  312.5 1.3 copy-done.8
  (49 shorter events, 5.1 us)
Async XLA Ops:
  7.2 12.2 %copy-start.2 = (f32[1024,512]{1,0:T(8,128)S(1)}, f32[1024,512]{1,0:T(8,128)}, u32[]{:S(2)}) copy-start(f32[1024,512]{1,0:T(8,128)} %param.23) | copy-start | bytes 6291460
  12.4 19.5 %all-to-all-start.5 = ((f32[16,16,512]{2,1,0:T(8,128)}), f32[16,16,512]{2,1,0:T(8,128)S(1)}, u32[]{:S(2)}, u32[]{:S(2)}) async-start(f32[16,16,512]{2,1,0:T(8,128)} %bitcast.149), calls=%async_computation.5 | async-start | bytes 1048576 | tf_op jit(solution)/shard_map/all_to_all | solution.py:394
  19.4 63.2 %collective-permute-start.18 = (f32[1024,512]{1,0:T(8,128)S(1)}, f32[1024,512]{1,0:T(8,128)}, u32[]{:S(2)}, u32[]{:S(2)}) collective-permute-start(f32[1024,512]{1,0:T(8,128)S(1)} %copy-done.2), channel_id=1, source_target_pairs={{0,256},{32,288},{64,320},{96,352},{128,384},{160,416},{192,448},{... | collective-permute-start | bytes 6291464 | tf_op jit(solution)/shard_map/ppermute | solution.py:20
  33.6 24.8 %all-to-all-start.6 = ((f32[4,16,768]{2,1,0:T(8,128)}), f32[4,16,768]{2,1,0:T(8,128)S(1)}, u32[]{:S(2)}, u32[]{:S(2)}) async-start(f32[4,16,768]{2,1,0:T(8,128)} %broadcast_in_dim.257), calls=%async_computation.6 | async-start | bytes 393216 | tf_op jit(solution)/shard_map/all_to_all | solution.py:37
  58.5 7.6 %collective-permute-start.7 = (f32[32,512]{1,0:T(8,128)S(1)}, f32[32,512]{1,0:T(8,128)S(1)}, u32[]{:S(2)}, u32[]{:S(2)}) collective-permute-start(f32[32,512]{1,0:T(8,128)S(1)} %pad_maximum_fusion.1), channel_id=1, source_target_pairs={{0,1},{1,0},{2,3},{3,2},{4,5},{5,4},{6,7},{7,6},{8,9},{9,8},{10,11... | collective-permute-start | bytes 196616 | tf_op jit(solution)/shard_map/cond/branch_1_fun/ppermute | solution.py:20
  76.1 22.7 %collective-permute-start.19 = (f32[64,512]{1,0:T(8,128)S(1)}, f32[64,512]{1,0:T(8,128)S(1)}, u32[]{:S(2)}, u32[]{:S(2)}) collective-permute-start(f32[64,512]{1,0:T(8,128)S(1)} %slice.864), channel_id=1, source_target_pairs={{0,0},{1,1},{2,32},{3,33},{4,64},{5,65},{6,96},{7,97},{8,128},{9,1... | collective-permute-start | bytes 393224 | tf_op jit(solution)/shard_map/ppermute | solution.py:334
  105.8 6.6 %collective-permute-start.2 = (f32[1024,512]{1,0:T(8,128)S(1)}, f32[1024,512]{1,0:T(8,128)S(1)}, u32[]{:S(2)}, u32[]{:S(2)}) collective-permute-start(f32[1024,512]{1,0:T(8,128)S(1)} %branch_1_fun.6.refs_0_), channel_id=1, source_target_pairs={{0,1},{1,0},{2,3},{3,2},{4,5},{5,4},{6,7},{7,6},{8,9},{9,8},{10,11... | collective-permute-start | bytes 6291464 | tf_op jit(solution)/shard_map/cond/branch_0_fun/cond/branch_1_fun/ppermute | solution.py:20
  116.0 192.9 %collective-permute-start.11 = (f32[1024,512]{1,0:T(8,128)}, f32[1024,512]{1,0:T(8,128)}, u32[]{:S(2)}, u32[]{:S(2)}) collective-permute-start(f32[1024,512]{1,0:T(8,128)} %get-tuple-element.169), channel_id=1, source_target_pairs={{0,16},{1,17},{2,18},{3,19},{4,20},{5,21},{6,22},{7,23},{8,24},{9,... | collective-permute-start | bytes 6291464 | tf_op jit(solution)/shard_map/cond/branch_0_fun/ppermute | solution.py:20
  133.3 13.9 %collective-permute-start.9 = (f32[256,512]{1,0:T(8,128)S(1)}, f32[256,512]{1,0:T(8,128)S(1)}, u32[]{:S(2)}, u32[]{:S(2)}) collective-permute-start(f32[256,512]{1,0:T(8,128)S(1)} %bitcast.323), channel_id=1, source_target_pairs={{0,1},{1,0},{2,3},{3,2},{4,5},{5,4},{6,7},{7,6},{8,9},{9,8},{10,11... | collective-permute-start | bytes 1572872 | tf_op jit(solution)/shard_map/cond/branch_0_fun/cond/branch_1_fun/ppermute | solution.py:20
  136.5 3.1 %collective-permute-start.10 = (f32[64,256]{1,0:T(8,128)S(1)}, f32[64,256]{1,0:T(8,128)S(1)}, u32[]{:S(2)}, u32[]{:S(2)}) collective-permute-start(f32[64,256]{1,0:T(8,128)S(1)} %slice_reduce_fusion), channel_id=1, source_target_pairs={{0,1},{1,0},{2,3},{3,2},{4,5},{5,4},{6,7},{7,6},{8,9},{9,8},{10,11... | collective-permute-start | bytes 196616 | tf_op jit(solution)/shard_map/cond/branch_0_fun/cond/branch_1_fun/ppermute | solution.py:20
  140.6 17.1 %all-to-all-start.1 = ((f32[4,64,768]{2,1,0:T(8,128)}), f32[4,64,768]{2,1,0:T(8,128)S(1)}, u32[]{:S(2)}, u32[]{:S(2)}) async-start(f32[4,64,768]{2,1,0:T(8,128)} %broadcast_in_dim.177), calls=%async_computation.1 | async-start | bytes 1572864 | tf_op jit(solution)/shard_map/cond/branch_0_fun/cond/branch_1_fun/all_to_all | solution.py:37
  312.5 1.3 copy-start.8

commit v5 on v4

--- a/solution.py
+++ b/solution.py
@@ -18,12 +18,6 @@
 def swap(value, axis, mask):
     pairs = [(source, source ^ mask) for source in range(lax.axis_size(axis))]
     return lax.ppermute(value, axis, pairs)
-
-
-def z_hi_groups():
-    size = lax.axis_size("col")
-    rest = size // Z_HI
-    return [list(range(low, size, rest)) for low in range(rest)]
 
 
 def gather(value, axis, stride, count):
@@ -437,18 +431,26 @@
         arrived = swap(moving, "col", top // col_blocks)
         return mine + arrived - close(quarter, flipped)
 
+    def send(field):
+        parts = [lax.dynamic_index_in_dim(field, z_hi ^ k) for k in range(1, Z_HI)]
+        return [swap(part, "col", k * cores * Y) for k, part in enumerate(parts, 1)]
+
+    def place(field, parts):
+        for k, part in enumerate(parts, 1):
+            field = lax.dynamic_update_slice(field, part, (z_hi ^ k, 0, 0))
+        return field
+
     def through(covariance, over, quarter, flipped, coef):
         plan = plans[3]
         mine, theirs = mix_rows(plan, covariance, over, coef)
         field = mine + swap(theirs, "row", plan.third // row_blocks)
+        field, quarter, flipped = lax.optimization_barrier((field, quarter, flipped))
         field = field.reshape(Z_HI, -1, cols_dev)
-        field = lax.all_to_all(field, "col", 0, 0, axis_index_groups=z_hi_groups())
-        field = mix_deep(plan, z_hi.astype(jnp.int32)[None], field, coef)
-        parts = [lax.dynamic_index_in_dim(field, z_hi ^ k) for k in range(Z_HI)]
-        parts[1:] = [swap(parts[k], "col", k * cores * Y) for k in range(1, Z_HI)]
+        parts = send(field)
         update = close(quarter, flipped)
-        for k, part in enumerate(parts):
-            field = lax.dynamic_update_slice(field, part, (z_hi ^ k, 0, 0))
+        parts, update = lax.optimization_barrier((parts, update))
+        field = mix_deep(plan, z_hi.astype(jnp.int32)[None], place(field, parts), coef)
+        field = place(field, lax.optimization_barrier(send(field)))
         return field.reshape(rows_dev, cols_dev) - update
 
     return lax.cond(index == 3, through, plain, covariance, over, quarter, flipped, coef)

time: 314 us -> 291 us (0.927)
  the two profiles are of different devices: /device:TPU:103 before, /device:TPU:37 now
where the time goes in v5:
time: 291 us
  waiting for transfers between devices  159 us (55%)
  starting transfers between devices  51.3 us (18%)
  Pallas kernels  32.8 us (11%)
  blocking collectives  23.7 us (8%)
  matrix products  9.33 us (3%)
  other arithmetic  7.74 us (3%)
  between operations  3.47 us (1%)
    ppermute x4, waiting for transfers between devices, swap(): return lax.ppermute(value, axis, pairs)  118 us
    pallas_call x1, Pallas kernels, solve_weights(): pl.pallas_call(weights_kernel, out_shape=jax.ShapeDtypeStruct(given.shape...  26 us
    all_to_all x2, blocking collectives, gather(): return lax.all_to_all(many, axis, 0, 0, axis_index_groups=groups)  23.7 us
    all_to_all x2, waiting for transfers between devices, gather(): return lax.all_to_all(many, axis, 0, 0, axis_index_groups=groups)  21.1 us
    all_to_all x2, starting transfers between devices, gather(): return lax.all_to_all(many, axis, 0, 0, axis_index_groups=groups)  19.6 us
    ppermute x4, starting transfers between devices, swap(): return lax.ppermute(value, axis, pairs)  15.1 us
    all_to_all x1, waiting for transfers between devices, shards(): spread = lax.all_to_all(part.reshape(n_row, -1, cols_dev), 'row', 0, 0)  9.93 us
    ppermute x1, waiting for transfers between devices, transposed(): return lax.ppermute(value, ('row', 'col'), pairs)  9.69 us
  transfers between devices with their start and end apart: 8, of which 6 were waited for; matrix products, arithmetic and copies ran while one was open for 3% of the time, Pallas kernels for 9%

profile of v5, /device:TPU:37, one launch (start us, length us, event | category | flops | bytes accessed | tf_op | source)
XLA Modules:
  0.0 290.8 jit_solution(16972211498448557340)
XLA Ops:
  0.0 1.3 and_select_fusion
  3.9 1.0 reshape.244.angles
  5.0 1.4 shard_map.48
  7.2 5.3 %fusion.10 = f32[256,512]{1,0:T(8,128)} fusion(f32[1024,512]{1,0:T(8,128)} %param.23, f32[1024]{0:T(1024)S(1)} %get-tuple-element.348, s32[1024]{0:T(1024)S(1)} %get-tuple-element.358, f32[1024]{0:T(1024)S(1)} %get-tuple-element.349, s32[1024]{0:T(1024)S(1)} %get-tuple-element.359, f32[1024]{0:T(1024)S(1)} %get-tuple-element.350, ...), kind=kOutput, calls=%fused_computation.185 | convolution fusion | flops 1616642048 | bytes 2688000 | tf_op jit(solution)/shard_map/dot_general | solution.py:387
  12.4 7.9 %all-to-all-start.4 = ((f32[16,16,512]{2,1,0:T(8,128)}), f32[16,16,512]{2,1,0:T(8,128)S(1)}, u32[]{:S(2)}, u32[]{:S(2)}) async-start(f32[16,16,512]{2,1,0:T(8,128)} %bitcast.149), calls=%async_computation.4 | async-start | bytes 1048576 | tf_op jit(solution)/shard_map/all_to_all | solution.py:388
  20.3 2.2 collective-permute-start.21
  22.6 9.9 %all-to-all-done.4 = f32[16,16,512]{2,1,0:T(8,128)S(1)} async-done(((f32[16,16,512]{2,1,0:T(8,128)}), f32[16,16,512]{2,1,0:T(8,128)S(1)}, u32[]{:S(2)}, u32[]{:S(2)}) %all-to-all-start.4) | async-done | bytes 524320 | tf_op jit(solution)/shard_map/all_to_all | solution.py:388
  32.6 0.9 fusion.34
  33.5 0.7 broadcast_in_dim.257
  34.2 12.1 %all-to-all-start.5 = ((f32[4,16,768]{2,1,0:T(8,128)}), f32[4,16,768]{2,1,0:T(8,128)S(1)}, u32[]{:S(2)}, u32[]{:S(2)}) async-start(f32[4,16,768]{2,1,0:T(8,128)} %broadcast_in_dim.257), calls=%async_computation.5 | async-start | bytes 393216 | tf_op jit(solution)/shard_map/all_to_all | solution.py:31
  46.3 12.6 %all-to-all-done.5 = f32[4,16,768]{2,1,0:T(8,128)S(1)} async-done(((f32[4,16,768]{2,1,0:T(8,128)}), f32[4,16,768]{2,1,0:T(8,128)S(1)}, u32[]{:S(2)}, u32[]{:S(2)}) %all-to-all-start.5) | async-done | bytes 196640 | tf_op jit(solution)/shard_map/all_to_all | solution.py:31
  58.9 0.2 conditional.8
  59.1 10.9 %all_to_all.33 = f32[4,16,768]{2,1,0:T(8,128)S(1)} all-to-all(f32[4,16,768]{2,1,0:T(8,128)S(1)} %broadcast_in_dim.258), channel_id=1, replica_groups={{0,32,64,96},{128,160,192,224},{256,288,320,352},{384,416,448,480},{1,3..., dimensions={0} | all-to-all | bytes 393216 | tf_op jit(solution)/shard_map/all_to_all | solution.py:31
  70.0 8.8 %collective-permute-start.22 = (f32[64,512]{1,0:T(8,128)S(1)}, f32[64,512]{1,0:T(8,128)S(1)}, u32[]{:S(2)}, u32[]{:S(2)}) collective-permute-start(f32[64,512]{1,0:T(8,128)S(1)} %slice.864), channel_id=1, source_target_pairs={{0,0},{1,1},{2,32},{3,33},{4,64},{5,65},{6,96},{7,97},{8,128},{9,1... | collective-permute-start | bytes 393224 | tf_op jit(solution)/shard_map/ppermute | solution.py:328
  78.8 9.7 %collective-permute-done.22 = f32[64,512]{1,0:T(8,128)S(1)} collective-permute-done((f32[64,512]{1,0:T(8,128)S(1)}, f32[64,512]{1,0:T(8,128)S(1)}, u32[]{:S(2)}, u32[]{:S(2)}) %collective-permute-start.22) | collective-permute-done | bytes 131104 | tf_op jit(solution)/shard_map/ppermute | solution.py:328
  88.5 202.3 %conditional.9 = (f32[1024,512]{1,0:T(8,128)}) conditional(s32[]{:T(128)} %convert_element_type.34, (s32[]{:T(128)}, f32[1024,512]{1,0:T(8,128)S(1)}, f32[1024,512]{1,0:T(8,128)}, f32[5,8,16,128]{3,2,1,0:T(8,128)S(1)}, s32[]{:T(128)}, /*index=5*/s32[1]{0:T(128)}, f32[64,768]{1,0:T(8,128)S(1)}, f32[64,512]{1,0:T(8,128)S(1)}) %tuple.256, (s32[]{:T(128)}, ...), branch_computations={%region_9.20_spmd, %region_20.24_spmd} | conditional | flops 1612873728 | bytes 93848472 | solution.py:456
  88.5 5.4 %conditional.3 = ((f32[1024,512]{1,0:T(8,128)}, f32[1024,512]{1,0:T(8,128)})) conditional(s32[]{:T(128)} %clamp.11, (f32[1024,512]{1,0:T(8,128)S(1)}, f32[1024,512]{1,0:T(8,128)}, f32[5,8,16,128]{3,2,1,0:T(8,128)S(1)}) %tuple.59, (f32[1024,512]{1,0:T(8,128)S(1)}, f32[1024,512]{1,0:T(8,128)}, ...), branch_computations={%region_10.10_spmd, %region_11.11_spmd, %region_12.16_spmd} | conditional | flops 524291 | bytes 39846080 | solution.py:426
  88.5 5.4 %branch_0_fun.1 = (f32[1024,512]{1,0:T(8,128)}, f32[1024,512]{1,0:T(8,128)}) custom-call(f32[1024,512]{1,0:T(8,128)S(1)} %get-tuple-element.149.near_ref, f32[1024,512]{1,0:T(8,128)} %get-tuple-element.150.top_ref, f32[5,8,16,128]{3,2,1,0:T(8,128)S(1)} %get-tuple-element.151.coef_ref), custom_call_target="tpu_custom_call" | custom-call | tf_op jit(solution)/shard_map/cond/branch_0_fun/cond/branch_0_fun/pallas_call | solution.py:229
  93.9 1.9 collective-permute-start.11
  96.4 72.7 %conditional.4 = (f32[1024,512]{1,0:T(8,128)}) conditional(s32[]{:T(128)} %bitcast.130, () %tuple.62, (f32[64,768]{1,0:T(8,128)S(1)}, f32[64,512]{1,0:T(8,128)S(1)}) %tuple.63), branch_computations={%region_17.17_spmd, %region_18.19_spmd} | conditional | flops 1611300864 | bytes 18350340 | solution.py:423
  96.6 12.8 %all_to_all.31 = f32[4,64,768]{2,1,0:T(8,128)S(1)} all-to-all(f32[4,64,768]{2,1,0:T(8,128)S(1)} %broadcast_in_dim.176), channel_id=1, replica_groups={{0,2,4,6},{1,3,5,7},{8,10,12,14},{9,11,13,15},{16,18,20,22},{17,19,21,2..., dimensions={0} | all-to-all | bytes 1572864 | tf_op jit(solution)/shard_map/cond/branch_0_fun/cond/branch_1_fun/all_to_all | solution.py:31
  109.4 9.0 %collective-permute-start.9 = (f32[256,512]{1,0:T(8,128)S(1)}, f32[256,512]{1,0:T(8,128)}, u32[]{:S(2)}, u32[]{:S(2)}) collective-permute-start(f32[256,512]{1,0:T(8,128)S(1)} %bitcast.324), channel_id=1, source_target_pairs={{0,1},{1,0},{2,3},{3,2},{4,5},{5,4},{6,7},{7,6},{8,9},{9,8},{10,11... | collective-permute-start | bytes 1572872 | tf_op jit(solution)/shard_map/cond/branch_0_fun/cond/branch_1_fun/ppermute | solution.py:20
  118.5 1.9 collective-permute-start.10
  120.4 1.2 collective-permute-done.10
  121.7 0.9 broadcast_in_dim.177
  122.6 7.5 %all-to-all-start.1 = ((f32[4,64,768]{2,1,0:T(8,128)}), f32[4,64,768]{2,1,0:T(8,128)S(1)}, u32[]{:S(2)}, u32[]{:S(2)}) async-start(f32[4,64,768]{2,1,0:T(8,128)} %broadcast_in_dim.177), calls=%async_computation.1 | async-start | bytes 1572864 | tf_op jit(solution)/shard_map/cond/branch_0_fun/cond/branch_1_fun/all_to_all | solution.py:31
  130.1 1.2 broadcast_select_fusion.1
  131.3 8.5 %all-to-all-done.1 = f32[4,64,768]{2,1,0:T(8,128)S(1)} async-done(((f32[4,64,768]{2,1,0:T(8,128)}), f32[4,64,768]{2,1,0:T(8,128)S(1)}, u32[]{:S(2)}, u32[]{:S(2)}) %all-to-all-start.1) | async-done | bytes 786464 | tf_op jit(solution)/shard_map/cond/branch_0_fun/cond/branch_1_fun/all_to_all | solution.py:31
  139.9 26.0 %branch_1_fun.8 = f32[256,512]{1,0:T(8,128)S(1)} custom-call(f32[256,256]{1,0:T(8,128)S(1)} %slice.840.square, f32[256,512]{1,0:T(8,128)S(1)} %slice.841.given), custom_call_target="tpu_custom_call" | custom-call | tf_op jit(solution)/shard_map/cond/branch_0_fun/cond/branch_1_fun/pallas_call | solution.py:292
  165.9 3.2 %fusion = f32[1024,512]{1,0:T(8,128)} fusion(f32[256,512]{1,0:T(8,128)S(1)} %branch_1_fun.8, f32[256,512]{1,0:T(8,128)S(1)} %get-tuple-element.330, f32[256,512]{1,0:T(8,128)S(1)} %get-tuple-element.329), kind=kOutput, calls=%fused_computation.151 | convolution fusion | flops 1610874880 | bytes 3670016 | tf_op jit(solution)/shard_map/cond/branch_0_fun/cond/branch_1_fun/dot_general | solution.py:417
  169.1 116.7 %collective-permute-done.11 = f32[1024,512]{1,0:T(8,128)} collective-permute-done((f32[1024,512]{1,0:T(8,128)}, f32[1024,512]{1,0:T(8,128)}, u32[]{:S(2)}, u32[]{:S(2)}) %collective-permute-start.11) | collective-permute-done | bytes 2097184 | tf_op jit(solution)/shard_map/cond/branch_0_fun/ppermute | solution.py:20
  285.9 4.9 %add_subtract_fusion = f32[1024,512]{1,0:T(8,128)} fusion(f32[1024,512]{1,0:T(8,128)} %get-tuple-element.385, f32[1024,512]{1,0:T(8,128)} %get-tuple-element.168, f32[1024,512]{1,0:T(8,128)} %collective-permute-done.11), kind=kLoop, calls=%fused_computation.161 | loop fusion | flops 1048576 | bytes 8388608 | tf_op jit(solution)/shard_map/cond/branch_0_fun/sub | solution.py:432
  (41 shorter events, 0.6 us)
Async XLA Ops:
  7.2 13.2 %copy-start.1 = (f32[1024,512]{1,0:T(8,128)S(1)}, f32[1024,512]{1,0:T(8,128)}, u32[]{:S(2)}) copy-start(f32[1024,512]{1,0:T(8,128)} %param.23) | copy-start | bytes 6291460
  12.4 20.1 %all-to-all-start.4 = ((f32[16,16,512]{2,1,0:T(8,128)}), f32[16,16,512]{2,1,0:T(8,128)S(1)}, u32[]{:S(2)}, u32[]{:S(2)}) async-start(f32[16,16,512]{2,1,0:T(8,128)} %bitcast.149), calls=%async_computation.4 | async-start | bytes 1048576 | tf_op jit(solution)/shard_map/all_to_all | solution.py:388
  20.3 58.5 %collective-permute-start.21 = (f32[1024,512]{1,0:T(8,128)S(1)}, f32[1024,512]{1,0:T(8,128)}, u32[]{:S(2)}, u32[]{:S(2)}) collective-permute-start(f32[1024,512]{1,0:T(8,128)S(1)} %copy-done.1), channel_id=1, source_target_pairs={{0,256},{32,288},{64,320},{96,352},{128,384},{160,416},{192,448},{... | collective-permute-start | bytes 6291464 | tf_op jit(solution)/shard_map/ppermute | solution.py:20
  34.2 24.7 %all-to-all-start.5 = ((f32[4,16,768]{2,1,0:T(8,128)}), f32[4,16,768]{2,1,0:T(8,128)S(1)}, u32[]{:S(2)}, u32[]{:S(2)}) async-start(f32[4,16,768]{2,1,0:T(8,128)} %broadcast_in_dim.257), calls=%async_computation.5 | async-start | bytes 393216 | tf_op jit(solution)/shard_map/all_to_all | solution.py:31
  70.0 18.5 %collective-permute-start.22 = (f32[64,512]{1,0:T(8,128)S(1)}, f32[64,512]{1,0:T(8,128)S(1)}, u32[]{:S(2)}, u32[]{:S(2)}) collective-permute-start(f32[64,512]{1,0:T(8,128)S(1)} %slice.864), channel_id=1, source_target_pairs={{0,0},{1,1},{2,32},{3,33},{4,64},{5,65},{6,96},{7,97},{8,128},{9,1... | collective-permute-start | bytes 393224 | tf_op jit(solution)/shard_map/ppermute | solution.py:328
  93.9 192.0 %collective-permute-start.11 = (f32[1024,512]{1,0:T(8,128)}, f32[1024,512]{1,0:T(8,128)}, u32[]{:S(2)}, u32[]{:S(2)}) collective-permute-start(f32[1024,512]{1,0:T(8,128)} %get-tuple-element.169), channel_id=1, source_target_pairs={{0,16},{1,17},{2,18},{3,19},{4,20},{5,21},{6,22},{7,23},{8,24},{9,... | collective-permute-start | bytes 6291464 | tf_op jit(solution)/shard_map/cond/branch_0_fun/ppermute | solution.py:20
  109.4 20.7 %collective-permute-start.9 = (f32[256,512]{1,0:T(8,128)S(1)}, f32[256,512]{1,0:T(8,128)}, u32[]{:S(2)}, u32[]{:S(2)}) collective-permute-start(f32[256,512]{1,0:T(8,128)S(1)} %bitcast.324), channel_id=1, source_target_pairs={{0,1},{1,0},{2,3},{3,2},{4,5},{5,4},{6,7},{7,6},{8,9},{9,8},{10,11... | collective-permute-start | bytes 1572872 | tf_op jit(solution)/shard_map/cond/branch_0_fun/cond/branch_1_fun/ppermute | solution.py:20
  118.5 3.1 %collective-permute-start.10 = (f32[64,256]{1,0:T(8,128)S(1)}, f32[64,256]{1,0:T(8,128)S(1)}, u32[]{:S(2)}, u32[]{:S(2)}) collective-permute-start(f32[64,256]{1,0:T(8,128)S(1)} %slice_reduce_fusion), channel_id=1, source_target_pairs={{0,1},{1,0},{2,3},{3,2},{4,5},{5,4},{6,7},{7,6},{8,9},{9,8},{10,11... | collective-permute-start | bytes 196616 | tf_op jit(solution)/shard_map/cond/branch_0_fun/cond/branch_1_fun/ppermute | solution.py:20
  122.6 17.2 %all-to-all-start.1 = ((f32[4,64,768]{2,1,0:T(8,128)}), f32[4,64,768]{2,1,0:T(8,128)S(1)}, u32[]{:S(2)}, u32[]{:S(2)}) async-start(f32[4,64,768]{2,1,0:T(8,128)} %broadcast_in_dim.177), calls=%async_computation.1 | async-start | bytes 1572864 | tf_op jit(solution)/shard_map/cond/branch_0_fun/cond/branch_1_fun/all_to_all | solution.py:31
